TPU v7x, 512 devices: a whole 4x4x16 slice. The times are simulated.
512 devices in a mesh: lat: 128 (over y, z, core), ens: 4 (over x).
Axes of the slice: x: 4, y: 4, z: 16, core: 2. Of those that a mesh axis runs over, the one named last changes fastest.
Arguments:
- background: bfloat16 [4, 128, 128, 384], P('ens', 'lat'), may hold values from -6 to 6
- increment: float32 [4, 128, 128, 384], P('ens', 'lat'), may hold values from -4 to 4
- residual: float32 [4, 128, 128, 384], P('ens', 'lat'), may hold values from -120 to 120
- direction: float32 [4, 128, 128, 384], P('ens', 'lat'), may hold values from -120 to 120
- spec_in: float32 [2, 8, 48, 48], replicated, may hold values from -0.625 to 0.625
- spec_out: float32 [2, 8, 48, 48], replicated, may hold values from -0.625 to 0.625
- mlp_in: bfloat16 [384, 3072], P(None, ('lat', 'ens')), may hold values from -0.3125 to 0.3125
- mlp_out: bfloat16 [3072, 384], P(('lat', 'ens')), may hold values from -0.109375 to 0.109375
- readout: float32 [384, 128], replicated, may hold values from -0.3125 to 0.3125
- obs_owner: int32 [16384, 1], P('lat'), may hold values from 0 to 127; in each aligned block of 128 rows (0 to 127, 128 to 255, ...) at most 2 rows name the same one
- obs_cell: int32 [16384], P('lat'), may hold values from 0 to 127
- obs_count: int32 [128], P('lat'), may hold values from 96 to 128, as said below
- obs_weight: float32 [16384, 128], P('lat'), may hold values from 0.5 to 8
Outputs:
- increment_new: float32 [4, 128, 128, 384], P('ens', 'lat')
- residual_new: float32 [4, 128, 128, 384], P('ens', 'lat')
- direction_new: float32 [4, 128, 128, 384], P('ens', 'lat')
- hessian_dir: float32 [4, 128, 128, 384], P('ens', 'lat')
Inputs may be any that keep to these rules, and one draw needn't show every extreme that they name: `obs_owner`: in the rows of one instrument owner, at most 2 refer to cells of one latitude owner. `obs_count`: rows of an instrument owner at or past its count carry no observation.
All inputs are finite; a program needn't handle non-finite values.
Results may differ from a plain program's by a relative error of at most 0.017.
Values may be sent and summed in bfloat16 or wider, within the bound.
A program may use at most 64 MiB of HBM per device.

v0:
```python
import math

import jax
import jax.numpy as jnp
from jax import lax
from jax.sharding import PartitionSpec as P

HIGHEST_PRECISION = lax.Precision.HIGHEST
NORM_EPSILON = 1e-05


def layer_norm(values):
    average = jnp.mean(values, axis=-1, keepdims=True)
    centred = values - average
    spread = jnp.mean(centred * centred, axis=-1, keepdims=True)
    return centred * lax.rsqrt(spread + NORM_EPSILON)


def gelu_value(values):
    return 0.5 * values * (1.0 + lax.erf(values * (1.0 / math.sqrt(2.0))))


def gelu_slope(values):
    cumulative = 0.5 * (1.0 + lax.erf(values * (1.0 / math.sqrt(2.0))))
    density = jnp.exp(-0.5 * values * values) * (1.0 / math.sqrt(2.0 * math.pi))
    return cumulative + values * density


def dft_tables(length):
    positions = jnp.arange(length, dtype=jnp.int32)
    products = positions[:, None] * positions[None, :] % length
    angles = products.astype(jnp.float32) * (2.0 * math.pi / length)
    norm_factor = 1.0 / math.sqrt(length)
    return (jnp.cos(angles) * norm_factor, jnp.sin(angles) * norm_factor)


def lon_forward(values_in, tables):
    cosine, sine_table = tables
    real_part = jnp.einsum("rjc,jl->rlc", values_in, cosine, precision=HIGHEST_PRECISION)
    imag_part = -jnp.einsum("rjc,jl->rlc", values_in, sine_table, precision=HIGHEST_PRECISION)
    return jnp.stack([real_part, imag_part])


def lon_inverse(field_pair, tables):
    cosine, sine_table = tables
    return jnp.einsum(
        "rlc,lj->rjc", field_pair[0], cosine, precision=HIGHEST_PRECISION
    ) - jnp.einsum("rlc,lj->rjc", field_pair[1], sine_table, precision=HIGHEST_PRECISION)


def lat_forward(field_pair, tables):
    cosine, sine_table = tables
    real_part = jnp.einsum(
        "ki,ilc->klc", cosine, field_pair[0], precision=HIGHEST_PRECISION
    ) + jnp.einsum("ki,ilc->klc", sine_table, field_pair[1], precision=HIGHEST_PRECISION)
    imag_part = jnp.einsum(
        "ki,ilc->klc", cosine, field_pair[1], precision=HIGHEST_PRECISION
    ) - jnp.einsum("ki,ilc->klc", sine_table, field_pair[0], precision=HIGHEST_PRECISION)
    return jnp.stack([real_part, imag_part])


def lat_inverse(field_pair, tables):
    cosine, sine_table = tables
    real_part = jnp.einsum(
        "ki,ilc->klc", cosine, field_pair[0], precision=HIGHEST_PRECISION
    ) - jnp.einsum("ki,ilc->klc", sine_table, field_pair[1], precision=HIGHEST_PRECISION)
    imag_part = jnp.einsum(
        "ki,ilc->klc", cosine, field_pair[1], precision=HIGHEST_PRECISION
    ) + jnp.einsum("ki,ilc->klc", sine_table, field_pair[0], precision=HIGHEST_PRECISION)
    return jnp.stack([real_part, imag_part])


def complex_mix(field_pair, weight):
    blocks = weight.shape[1]
    block_size = weight.shape[2]
    shaped = field_pair.reshape(field_pair.shape[:-1] + (blocks, block_size))
    real_part = jnp.einsum(
        "...bd,bde->...be", shaped[0], weight[0], precision=HIGHEST_PRECISION
    ) - jnp.einsum("...bd,bde->...be", shaped[1], weight[1], precision=HIGHEST_PRECISION)
    imag_part = jnp.einsum(
        "...bd,bde->...be", shaped[1], weight[0], precision=HIGHEST_PRECISION
    ) + jnp.einsum("...bd,bde->...be", shaped[0], weight[1], precision=HIGHEST_PRECISION)
    return jnp.stack([real_part, imag_part]).reshape(field_pair.shape)


def complex_mix_adjoint(field_pair, weight):
    blocks = weight.shape[1]
    block_size = weight.shape[2]
    shaped = field_pair.reshape(field_pair.shape[:-1] + (blocks, block_size))
    real_part = jnp.einsum(
        "...be,bde->...bd", shaped[0], weight[0], precision=HIGHEST_PRECISION
    ) + jnp.einsum("...be,bde->...bd", shaped[1], weight[1], precision=HIGHEST_PRECISION)
    imag_part = jnp.einsum(
        "...be,bde->...bd", shaped[1], weight[0], precision=HIGHEST_PRECISION
    ) - jnp.einsum("...be,bde->...bd", shaped[0], weight[1], precision=HIGHEST_PRECISION)
    return jnp.stack([real_part, imag_part]).reshape(field_pair.shape)


def contract(left_rows, weight, flipped):
    if flipped:
        return lax.dot_general(
            left_rows, weight, (((1,), (1,)), ((), ())), preferred_element_type=jnp.float32
        )
    return jnp.dot(left_rows, weight, preferred_element_type=jnp.float32)


def to_spectral(field_pair):
    return lax.all_to_all(
        field_pair.astype(jnp.bfloat16), "lat", split_axis=2, concat_axis=1, tiled=True
    ).astype(field_pair.dtype)


def to_grid(field_pair):
    return lax.all_to_all(
        field_pair.astype(jnp.bfloat16), "lat", split_axis=1, concat_axis=2, tiled=True
    ).astype(field_pair.dtype)


def per_device(
    background,
    increment,
    residual,
    direction,
    spec_in,
    spec_out,
    mlp_in,
    mlp_out,
    readout,
    obs_owner,
    obs_cell,
    obs_count,
    obs_weight,
):
    lat_groups = lax.axis_size("lat")
    band_rows = background.shape[1]
    lon_cells = background.shape[2]
    features = background.shape[3]
    grid_cells = band_rows * lon_cells
    obs_rows = obs_owner.shape[0]
    capacity = 2 * obs_rows // lat_groups
    lon_tables = dft_tables(lon_cells)
    lat_tables = dft_tables(band_rows * lat_groups)
    norm_now = lax.psum(jnp.sum(residual * residual), ("lat", "ens"))
    first_weight, second_weight = (
        lax.all_gather(mlp_in, ("lat", "ens"), axis=1, tiled=True),
        lax.all_gather(mlp_out, ("lat", "ens"), axis=0, tiled=True),
    )
    owners = obs_owner[:, 0]
    onehot = (owners[:, None] == jnp.arange(lat_groups, dtype=jnp.int32)[None, :]).astype(jnp.int32)
    earlier = jnp.cumsum(onehot, axis=0) - onehot
    placing = owners * capacity + jnp.sum(earlier * onehot, axis=1)
    requests = jnp.zeros((lat_groups * capacity,), jnp.int32).at[placing].set(obs_cell)
    asked_cells = lax.all_to_all(
        requests.reshape(lat_groups, capacity), "lat", split_axis=0, concat_axis=0, tiled=True
    ).reshape(lat_groups * capacity)
    observed = jnp.arange(obs_rows, dtype=jnp.int32) < obs_count[0]
    weights = jnp.where(observed[:, None], obs_weight, 0.0)
    state_field = background[0].astype(jnp.float32)
    heading = direction[0]
    normed, first_pull = jax.vjp(layer_norm, state_field)
    spectrum = lat_forward(to_spectral(lon_forward(normed, lon_tables)), lat_tables)
    before = complex_mix(spectrum, spec_in)
    spec_slope = gelu_slope(before)
    filtered = lon_inverse(
        to_grid(lat_inverse(complex_mix(gelu_value(before), spec_out), lat_tables)), lon_tables
    )
    middle = state_field + filtered
    mixed_norm, second_pull = jax.vjp(layer_norm, middle)
    mixed_low = mixed_norm.reshape(grid_cells, features).astype(jnp.bfloat16)
    tangent_normed = jax.jvp(layer_norm, (state_field,), (heading,))[1]
    tangent_spec = complex_mix(
        lat_forward(to_spectral(lon_forward(tangent_normed, lon_tables)), lat_tables), spec_in
    )
    tangent_filtered = lon_inverse(
        to_grid(lat_inverse(complex_mix(spec_slope * tangent_spec, spec_out), lat_tables)),
        lon_tables,
    )
    tangent_middle = heading + tangent_filtered
    tangent_mixed = (
        jax.jvp(layer_norm, (middle,), (tangent_middle,))[1]
        .reshape(grid_cells, features)
        .astype(jnp.bfloat16)
    )
    mlp_slope = gelu_slope(contract(mixed_low, first_weight, False))
    tangent_hidden = (mlp_slope * contract(tangent_mixed, first_weight, False)).astype(jnp.bfloat16)
    tangent_added = contract(tangent_hidden, second_weight, False)
    tangent_out = tangent_middle.reshape(grid_cells, features) + tangent_added
    found_rows = tangent_out[asked_cells].reshape(lat_groups, capacity, features)
    returned = (
        lax.all_to_all(
            found_rows.astype(jnp.bfloat16), "lat", split_axis=0, concat_axis=0, tiled=True
        )
        .astype(found_rows.dtype)
        .reshape(lat_groups * capacity, features)
    )
    departures = jnp.dot(returned[placing], readout, precision=HIGHEST_PRECISION)
    pulled = jnp.dot(weights * departures, readout.T, precision=HIGHEST_PRECISION)
    outgoing = jnp.zeros((lat_groups * capacity, features), jnp.float32).at[placing].set(pulled)
    arrived = (
        lax.all_to_all(
            outgoing.reshape(lat_groups, capacity, features).astype(jnp.bfloat16),
            "lat",
            split_axis=0,
            concat_axis=0,
            tiled=True,
        )
        .astype(jnp.float32)
        .reshape(lat_groups * capacity, features)
    )
    gradient = jnp.zeros((grid_cells, features), jnp.float32).at[asked_cells].add(arrived)
    gradient_low = gradient.astype(jnp.bfloat16)
    grad_pre = (mlp_slope * contract(gradient_low, second_weight, True)).astype(jnp.bfloat16)
    grad_mixed = contract(grad_pre, first_weight, True)
    grad_middle = (
        gradient.reshape(band_rows, lon_cells, features)
        + second_pull(grad_mixed.reshape(band_rows, lon_cells, features))[0]
    )
    grad_spec = spec_slope * complex_mix_adjoint(
        lat_forward(to_spectral(lon_forward(grad_middle, lon_tables)), lat_tables), spec_out
    )
    grad_normed = lon_inverse(
        to_grid(lat_inverse(complex_mix_adjoint(grad_spec, spec_in), lat_tables)), lon_tables
    )
    hessian_dir = (heading + grad_middle + first_pull(grad_normed)[0])[None]
    curvature = lax.psum(jnp.sum(direction * hessian_dir), ("lat", "ens"))
    step_size = norm_now / curvature
    increment_new = increment + step_size * direction
    residual_new = residual - step_size * hessian_dir
    norm_next = lax.psum(jnp.sum(residual_new * residual_new), ("lat", "ens"))
    direction_new = residual_new + norm_next / norm_now * direction
    return (increment_new, residual_new, direction_new, hessian_dir)


def solution(mesh):
    return jax.shard_map(
        per_device,
        mesh=mesh,
        in_specs=(
            P("ens", "lat", None, None),
            P("ens", "lat", None, None),
            P("ens", "lat", None, None),
            P("ens", "lat", None, None),
            P(),
            P(),
            P(None, ("lat", "ens")),
            P(("lat", "ens"), None),
            P(),
            P("lat", None),
            P("lat"),
            P("lat"),
            P("lat", None),
        ),
        out_specs=(
            P("ens", "lat", None, None),
            P("ens", "lat", None, None),
            P("ens", "lat", None, None),
            P("ens", "lat", None, None),
        ),
        check_vma=False,
    )
```

profile of v0, /device:TPU:1, one launch (start us, length us, event | category | flops | bytes accessed | tf_op | source)
XLA Modules:
  0.0 784.2 jit_solution(10519243111763776039)
XLA Ops:
  10.4 1.1 scatter_custom_fusion
  12.2 20.6 %all-to-all-start = ((s32[128,1,2]{2,1,0:T(1,128)}), s32[128,1,2]{2,1,0:T(1,128)S(1)}, u32[]{:S(2)}, u32[]{:S(2)}) async-start(s32[128,1,2]{2,1,0:T(1,128)} %bitcast.4), calls=%async_computation | async-start | bytes 131072 | tf_op jit(solution)/shard_map/all_to_all | solution.py:153
  32.8 1.0 reduce_sum.153
  33.8 1.0 convert_reduce_fusion
  34.9 1.2 fusion.49
  36.6 1.5 fusion.20
  38.1 1.5 fusion.25
  39.7 0.9 copy.122
  40.6 7.2 all-to-all-done
  47.8 9.0 %all-to-all-start.1 = ((bf16[2,1,128,384]{3,0,1,2:T(2,128)(2,1)}), bf16[2,1,128,384]{3,0,1,2:T(2,128)(2,1)S(1)}, u32[]{:S(2)}, u32[]{:S(2)}) async-start(bf16[2,1,128,384]{3,0,1,2:T(2,128)(2,1)} %copy.122), calls=%async_computation.1 | async-start | bytes 393216 | tf_op jit(solution)/shard_map/all_to_all | solution.py:108
  58.9 0.9 copy.129
  61.3 15.3 %all-to-all-done.1 = bf16[2,1,128,384]{3,0,1,2:T(2,128)(2,1)S(1)} async-done(((bf16[2,1,128,384]{3,0,1,2:T(2,128)(2,1)}), bf16[2,1,128,384]{3,0,1,2:T(2,128)(2,1)S(1)}, u32[]{:S(2)}, u32[]{:S(2)}) %all-to-all-start.1) | async-done | bytes 196640 | tf_op jit(solution)/shard_map/all_to_all | solution.py:108
  76.6 7.5 all-to-all-start.2
  88.6 15.3 %all-to-all-done.2 = bf16[2,1,128,384]{3,0,1,2:T(2,128)(2,1)S(1)} async-done(((bf16[2,1,128,384]{3,0,1,2:T(2,128)(2,1)}), bf16[2,1,128,384]{3,0,1,2:T(2,128)(2,1)S(1)}, u32[]{:S(2)}, u32[]{:S(2)}) %all-to-all-start.2) | async-done | bytes 196640 | tf_op jit(solution)/shard_map/all_to_all | solution.py:108
  113.4 1.3 copy.139
  114.7 7.1 all-to-all-start.4
  126.4 0.9 copy.136
  127.3 15.0 %all-to-all-done.4 = bf16[2,128,1,384]{3,0,2,1:T(2,128)(2,1)S(1)} async-done(((bf16[2,128,1,384]{3,0,2,1:T(2,128)(2,1)}), bf16[2,128,1,384]{3,0,2,1:T(2,128)(2,1)S(1)}, u32[]{:S(2)}, u32[]{:S(2)}) %all-to-all-start.4) | async-done | bytes 196640 | tf_op jit(solution)/shard_map/all_to_all | solution.py:114
  142.2 7.2 all-to-all-start.3
  150.9 18.5 %all-to-all-done.3 = bf16[2,128,1,384]{3,0,2,1:T(2,128)(2,1)S(1)} async-done(((bf16[2,128,1,384]{3,0,2,1:T(2,128)(2,1)}), bf16[2,128,1,384]{3,0,2,1:T(2,128)(2,1)S(1)}, u32[]{:S(2)}, u32[]{:S(2)}) %all-to-all-start.3) | async-done | bytes 196640 | tf_op jit(solution)/shard_map/all_to_all | solution.py:114
  172.3 43.9 %all-gather.5.cloned.1.call-done = bf16[512,6,384]{2,1,0:T(8,128)(2,1)} async-done(((bf16[1,6,384]{2,1,0:T(8,128)(2,1)}), bf16[512,6,384]{2,1,0:T(8,128)(2,1)}) %all-gather.5.cloned.1.call-update) | async-done | bytes 2359312 | tf_op jit(solution)/shard_map/all_gather | solution.py:145
  216.2 3.8 reshape.1505
  220.0 2.8 fusion.5
  222.8 188.8 %all-gather.7.cloned.1.call-done = bf16[512,6,384]{2,1,0:T(8,128)(2,1)} async-done(((bf16[1,6,384]{2,1,0:T(8,128)(2,1)}), bf16[512,6,384]{2,1,0:T(8,128)(2,1)}) %all-gather.7.cloned.1.call-update) | async-done | bytes 2359312 | tf_op jit(solution)/shard_map/all_gather | solution.py:146
  411.7 5.2 reshape.1507
  416.9 3.6 fusion.10
  420.5 1.8 gather_fusion
  422.3 1.7 convert_element_type.209
  424.0 11.0 %all-to-all-start.5 = ((bf16[128,2,384]{2,1,0:T(2,128)(2,1)}), bf16[128,2,384]{2,1,0:T(2,128)(2,1)}, u32[]{:S(2)}, u32[]{:S(2)}) async-start(bf16[128,2,384]{2,1,0:T(2,128)(2,1)} %convert_element_type.209), calls=%async_computation.5 | async-start | bytes 393216 | tf_op jit(solution)/shard_map/all_to_all | solution.py:190
  436.2 18.4 %all-to-all-done.5 = bf16[128,2,384]{2,1,0:T(2,128)(2,1)} async-done(((bf16[128,2,384]{2,1,0:T(2,128)(2,1)}), bf16[128,2,384]{2,1,0:T(2,128)(2,1)}, u32[]{:S(2)}, u32[]{:S(2)}) %all-to-all-start.5) | async-done | bytes 196640 | tf_op jit(solution)/shard_map/all_to_all | solution.py:190
  454.6 1.0 reshape.1448
  455.6 1.5 gather_fusion.1
  457.1 1.2 convolution_multiply_fusion.2
  458.3 1.0 fusion.360
  459.3 2.1 scatter_custom_fusion.1
  461.4 1.7 convert_element_type.210
  463.1 1.7 convert_element_type.211
  464.8 28.8 %all_to_all.73 = bf16[128,2,384]{2,1,0:T(2,128)(2,1)} all-to-all(bf16[128,2,384]{2,1,0:T(2,128)(2,1)} %convert_element_type.211), channel_id=1, replica_groups=mesh['lat'=128,'ens'=4] {'lat'}, dimensions={0} | all-to-all | bytes 393216 | tf_op jit(solution)/shard_map/all_to_all | solution.py:200
  493.6 1.7 reshape.1500
  495.4 3.2 scatter_custom_fusion.2
  498.6 4.6 multiply_reduce_fusion.3
  503.9 1.1 fusion.346
  505.0 1.0 add_add_fusion.2
  507.5 26.0 %all_to_all.74 = bf16[2,1,128,384]{3,0,1,2:T(2,128)(2,1)S(1)} all-to-all(bf16[2,1,128,384]{3,0,1,2:T(2,128)(2,1)S(1)} %copy.142), channel_id=1, replica_groups=mesh['lat'=128,'ens'=4] {'lat'}, dimensions={2} | all-to-all | bytes 393216 | tf_op jit(solution)/shard_map/all_to_all | solution.py:108
  542.2 7.1 all-to-all-start.8
  550.0 19.4 %all-to-all-done.8 = bf16[2,128,1,384]{3,0,2,1:T(2,128)(2,1)S(1)} async-done(((bf16[2,128,1,384]{3,0,2,1:T(2,128)(2,1)}), bf16[2,128,1,384]{3,0,2,1:T(2,128)(2,1)S(1)}, u32[]{:S(2)}, u32[]{:S(2)}) %all-to-all-start.8) | async-done | bytes 196640 | tf_op jit(solution)/shard_map/all_to_all | solution.py:114
  572.0 101.3 %all-reduce = (f32[]{:T(128)}, f32[]{:T(128)}) all-reduce(f32[]{:T(128)} %multiply_reduce_fusion.5, f32[]{:T(128)} %multiply_reduce_fusion.2), channel_id=1, replica_groups=mesh['lat'=128,'ens'=4] {'lat','ens'}, use_global_device_ids=true, to_apply=%region_1.2 | all-reduce | flops 2 | bytes 16 | tf_op jit(solution)/shard_map/psum | solution.py:143
  675.2 99.6 %psum.23 = f32[]{:T(128)} all-reduce(f32[]{:T(128)} %get-tuple-element.10), channel_id=1, replica_groups=mesh['lat'=128,'ens'=4] {'lat','ens'}, use_global_device_ids=true, to_apply=%region_22.23 | all-reduce | flops 1 | bytes 8 | tf_op jit(solution)/shard_map/psum | solution.py:229
  (171 shorter events, 46.3 us)
Async XLA Ops:
  7.2 449.9 %copy-start = (f32[384,128]{1,0:T(8,128)S(1)}, f32[384,128]{1,0:T(8,128)}, u32[]{:S(2)}) copy-start(f32[384,128]{1,0:T(8,128)} %param.21) | copy-start | bytes 589828
  7.2 209.0 %all-gather.5.cloned.1.call-start = ((), (), s32[]{:S(2)}) async-start(), calls=%async_computation.9 | async-start | bytes 3151872 | tf_op jit(solution)/shard_map/all_gather | solution.py:145
  8.7 48.9 %copy-start.3 = (f32[1,1,128,384]{3,2,1,0:T(8,128)S(1)}, f32[1,1,128,384]{3,2,1,0:T(8,128)}, u32[]{:S(2)}) copy-start(f32[1,1,128,384]{3,2,1,0:T(8,128)} %param.16) | copy-start | bytes 589828
  8.7 48.9 %copy-start.8 = (bf16[1,1,128,384]{3,2,1,0:T(8,128)(2,1)S(1)}, bf16[1,1,128,384]{3,2,1,0:T(8,128)(2,1)}, u32[]{:S(2)}) copy-start(bf16[1,1,128,384]{3,2,1,0:T(8,128)(2,1)} %param.13) | copy-start | bytes 294916
  10.4 27.8 %copy-start.26 = (s32[128]{0:T(128)}, s32[128]{0:T(128)S(1)}, u32[]{:S(2)}) copy-start(s32[128]{0:T(128)S(1)} %fusion.158) | copy-start | bytes 1540
  12.2 35.5 %all-to-all-start = ((s32[128,1,2]{2,1,0:T(1,128)}), s32[128,1,2]{2,1,0:T(1,128)S(1)}, u32[]{:S(2)}, u32[]{:S(2)}) async-start(s32[128,1,2]{2,1,0:T(1,128)} %bitcast.4), calls=%async_computation | async-start | bytes 131072 | tf_op jit(solution)/shard_map/all_to_all | solution.py:153
  47.8 28.8 %all-to-all-start.1 = ((bf16[2,1,128,384]{3,0,1,2:T(2,128)(2,1)}), bf16[2,1,128,384]{3,0,1,2:T(2,128)(2,1)S(1)}, u32[]{:S(2)}, u32[]{:S(2)}) async-start(bf16[2,1,128,384]{3,0,1,2:T(2,128)(2,1)} %copy.122), calls=%async_computation.1 | async-start | bytes 393216 | tf_op jit(solution)/shard_map/all_to_all | solution.py:108
  56.8 354.9 %all-gather.7.cloned.1.call-start = ((), (), s32[]{:S(2)}) async-start(), calls=%async_computation.10 | async-start | bytes 3151872 | tf_op jit(solution)/shard_map/all_gather | solution.py:146
  59.8 26.2 %copy-start.2 = (f32[2,8,48,48]{3,2,1,0:T(8,128)S(1)}, f32[2,8,48,48]{3,2,1,0:T(8,128)}, u32[]{:S(2)}) copy-start(f32[2,8,48,48]{3,2,1,0:T(8,128)} %param.17) | copy-start | bytes 442372
  61.2 15.3 %copy-start.21 = (s32[256,1]{0,1:T(1,128)}, s32[256,1]{0,1:T(1,128)S(1)}, u32[]{:S(2)}) copy-start(s32[256,1]{0,1:T(1,128)S(1)} %compare_select_fusion) | copy-start | bytes 3076
  76.6 27.3 %all-to-all-start.2 = ((bf16[2,1,128,384]{3,0,1,2:T(2,128)(2,1)}), bf16[2,1,128,384]{3,0,1,2:T(2,128)(2,1)S(1)}, u32[]{:S(2)}, u32[]{:S(2)}) async-start(bf16[2,1,128,384]{3,0,1,2:T(2,128)(2,1)} %copy.129), calls=%async_computation.2 | async-start | bytes 393216 | tf_op jit(solution)/shard_map/all_to_all | solution.py:108
  88.0 20.4 %copy-start.11 = (f32[8,128,48]{1,2,0:T(8,128)}, f32[8,128,48]{1,2,0:T(8,128)S(1)}, u32[]{:S(2)}) copy-start(f32[8,128,48]{1,2,0:T(8,128)S(1)} %convolution_subtract_fusion.14) | copy-start | bytes 589828
  88.5 19.9 %copy-start.13 = (f32[8,128,48]{1,2,0:T(8,128)}, f32[8,128,48]{1,2,0:T(8,128)S(1)}, u32[]{:S(2)}) copy-start(f32[8,128,48]{1,2,0:T(8,128)S(1)} %convolution_add_fusion.11) | copy-start | bytes 589828
  107.9 1.0 copy-start.1
  114.7 27.5 %all-to-all-start.4 = ((bf16[2,128,1,384]{3,0,2,1:T(2,128)(2,1)}), bf16[2,128,1,384]{3,0,2,1:T(2,128)(2,1)S(1)}, u32[]{:S(2)}, u32[]{:S(2)}) async-start(bf16[2,128,1,384]{3,0,2,1:T(2,128)(2,1)} %copy.139), calls=%async_computation.4 | async-start | bytes 393216 | tf_op jit(solution)/shard_map/all_to_all | solution.py:114
  142.2 27.1 %all-to-all-start.3 = ((bf16[2,128,1,384]{3,0,2,1:T(2,128)(2,1)}), bf16[2,128,1,384]{3,0,2,1:T(2,128)(2,1)S(1)}, u32[]{:S(2)}, u32[]{:S(2)}) async-start(bf16[2,128,1,384]{3,0,2,1:T(2,128)(2,1)} %copy.136), calls=%async_computation.3 | async-start | bytes 393216 | tf_op jit(solution)/shard_map/all_to_all | solution.py:114
  150.9 21.4 %copy-start.5 = (f32[128,384]{1,0:T(8,128)}, f32[128,384]{1,0:T(8,128)S(1)}, u32[]{:S(2)}) copy-start(f32[128,384]{1,0:T(8,128)S(1)} %get-tuple-element.45) | copy-start | bytes 589828
  170.8 0.7 copy-start.10
  170.8 1.5 copy-start.22
  216.2 3.8 copy-start.6
  222.8 194.0 %copy-start.19 = (f32[128]{0:T(128)S(1)}, f32[128]{0:T(128)}, u32[]{:S(2)}) copy-start(f32[128]{0:T(128)} %get-tuple-element.40) | copy-start | bytes 1540
  222.8 194.0 %copy-start.23 = (f32[128]{0:T(128)S(1)}, f32[128]{0:T(128)}, u32[]{:S(2)}) copy-start(f32[128]{0:T(128)} %copy-done.22) | copy-start | bytes 1540
  222.8 194.0 %copy-start.24 = (f32[128]{0:T(128)S(1)}, f32[128]{0:T(128)}, u32[]{:S(2)}) copy-start(f32[128]{0:T(128)} %get-tuple-element.14) | copy-start | bytes 1540
  420.5 15.7 %copy-start.27 = (s32[128]{0:T(128)S(1)}, s32[128]{0:T(128)}, u32[]{:S(2)}) copy-start(s32[128]{0:T(128)} %copy-done.26) | copy-start | bytes 1540
  424.0 30.6 %all-to-all-start.5 = ((bf16[128,2,384]{2,1,0:T(2,128)(2,1)}), bf16[128,2,384]{2,1,0:T(2,128)(2,1)}, u32[]{:S(2)}, u32[]{:S(2)}) async-start(bf16[128,2,384]{2,1,0:T(2,128)(2,1)} %convert_element_type.209), calls=%async_computation.5 | async-start | bytes 393216 | tf_op jit(solution)/shard_map/all_to_all | solution.py:190
  458.2 40.3 %copy-start.7 = (f32[128,384]{1,0:T(8,128)S(1)}, f32[128,384]{1,0:T(8,128)}, u32[]{:S(2)}) copy-start(f32[128,384]{1,0:T(8,128)} %copy-done.5) | copy-start | bytes 589828
  498.6 5.3 copy-start.20
  535.8 1.4 copy-start.12
  535.9 1.4 copy-start.14
  538.8 10.6 %copy-start.16 = (f32[1,1,128,384]{3,2,1,0:T(8,128)S(1)}, f32[1,1,128,384]{3,2,1,0:T(8,128)}, u32[]{:S(2)}) copy-start(f32[1,1,128,384]{3,2,1,0:T(8,128)} %param.15) | copy-start | bytes 589828
  540.7 29.6 %copy-start.9 = (bf16[1,1,128,384]{3,2,1,0:T(8,128)(2,1)S(1)}, bf16[1,1,128,384]{3,2,1,0:T(8,128)(2,1)}, u32[]{:S(2)}) copy-start(bf16[1,1,128,384]{3,2,1,0:T(8,128)(2,1)} %param.13) | copy-start | bytes 294916
  541.3 29.6 %copy-start.25 = (f32[128]{0:T(128)S(1)}, f32[128]{0:T(128)}, u32[]{:S(2)}) copy-start(f32[128]{0:T(128)} %get-tuple-element.17) | copy-start | bytes 1540
  541.3 29.8 %copy-start.4 = (f32[1,1,128,384]{3,2,1,0:T(8,128)S(1)}, f32[1,1,128,384]{3,2,1,0:T(8,128)}, u32[]{:S(2)}) copy-start(f32[1,1,128,384]{3,2,1,0:T(8,128)} %param.16) | copy-start | bytes 589828
  542.2 27.2 %all-to-all-start.8 = ((bf16[2,128,1,384]{3,0,2,1:T(2,128)(2,1)}), bf16[2,128,1,384]{3,0,2,1:T(2,128)(2,1)S(1)}, u32[]{:S(2)}, u32[]{:S(2)}) async-start(bf16[2,128,1,384]{3,0,2,1:T(2,128)(2,1)} %copy.155), calls=%async_computation.8 | async-start | bytes 393216 | tf_op jit(solution)/shard_map/all_to_all | solution.py:114
  569.7 206.5 %copy-start.18 = (f32[1,1,128,384]{3,2,1,0:T(8,128)S(1)}, f32[1,1,128,384]{3,2,1,0:T(8,128)}, u32[]{:S(2)}) copy-start(f32[1,1,128,384]{3,2,1,0:T(8,128)} %param.14) | copy-start | bytes 589828
  571.3 205.7 %copy-start.15 = (f32[128,384]{1,0:T(8,128)}, f32[128,384]{1,0:T(8,128)S(1)}, u32[]{:S(2)}) copy-start(f32[128,384]{1,0:T(8,128)S(1)} %fusion.88) | copy-start | bytes 589828
  675.2 101.8 %copy-start.17 = (f32[1,1,128,384]{3,2,1,0:T(8,128)}, f32[1,1,128,384]{3,2,1,0:T(8,128)S(1)}, u32[]{:S(2)}) copy-start(f32[1,1,128,384]{3,2,1,0:T(8,128)S(1)} %get-tuple-element.11) | copy-start | bytes 589828
Sparse Core Ops, SparseCore 0:
  12.4 203.7 all-gather.4
  220.6 191.0 all-gather.6
where the time goes:
time: 793 us; the launch traced here: 784 us
  waiting for transfers between devices  343 us (43%)
  blocking collectives  256 us (32%)
  starting transfers between devices  69.5 us (9%)
  matrix products  45.8 us (6%)
  local copies, waits for them, and re-layouts  31.6 us (4%)
  other arithmetic  19.6 us (2%)
  between operations  18.8 us (2%)
    all_gather x1, waiting for transfers between devices, per_device(): lax.all_gather(mlp_out, ('lat', 'ens'), axis=0, tiled=True)  189 us
    psum x1, blocking collectives, per_device(): norm_now = lax.psum(jnp.sum(residual * residual), ('lat', 'ens'))  101 us
    psum x1, blocking collectives, per_device(): norm_next = lax.psum(jnp.sum(residual_new * residual_new), ('lat', 'ens'))  99.6 us
    all_to_all x3, waiting for transfers between devices, to_grid(): lax.all_to_all(field_pair.astype(jnp.bfloat16), 'lat', split_axis=1, conc...  52.9 us
    all_gather x1, waiting for transfers between devices, per_device(): lax.all_gather(mlp_in, ('lat', 'ens'), axis=1, tiled=True)  43.9 us
    all_to_all x2, waiting for transfers between devices, to_spectral(): lax.all_to_all(field_pair.astype(jnp.bfloat16), 'lat', split_axis=2, conc...  30.6 us
    all_to_all x1, blocking collectives, per_device(): lax.all_to_all(outgoing.reshape(lat_groups, capacity, features).astype(jn...  28.8 us
    all_to_all x1, blocking collectives, to_spectral(): lax.all_to_all(field_pair.astype(jnp.bfloat16), 'lat', split_axis=2, conc...  26 us
  transfers between devices with their start and end apart: 9, of which 9 were waited for; matrix products, arithmetic and copies ran while one was open for 6% of the time, Pallas kernels for 0%

commit v1 on v0

v1 whole, which is shorter than its diff:
```python
import functools
import math

import jax
import jax.numpy as jnp
import numpy as np
from jax import lax
from jax.experimental import pallas as pl
from jax.experimental.pallas import tpu as pltpu
from jax.sharding import PartitionSpec as P

MESH = pl.DeviceIdType.MESH
F32 = jnp.float32
BF16 = jnp.bfloat16
NORM_EPSILON = 1e-05
FEATURES = 384
BLOCK = 48
FIELDS = 7


def split_np(table):
    high = table.astype(np.float32).astype(jnp.bfloat16)
    low = (table - high.astype(np.float64)).astype(np.float32).astype(jnp.bfloat16)
    return high, low


def make_tables(ny, nz):
    chips = ny * nz
    n = 2 * chips
    scale = 1.0 / math.sqrt(n)
    pos = np.arange(n)
    angle = 2.0 * math.pi * ((pos[:, None] * pos[None, :]) % n) / n
    cosine, sine = np.cos(angle) * scale, np.sin(angle) * scale
    alternate = np.where(pos % 2 == 0, 1.0, -1.0) * scale
    lon_f = np.concatenate([cosine[:chips], -sine[:chips]], 0)
    lon_f[chips] = alternate
    y, z, a = np.meshgrid(np.arange(ny), np.arange(nz), np.arange(2), indexing="ij")
    row = (y * nz + z) * 2 + a
    arrive = row.transpose(1, 0, 2).reshape(-1)
    depart = row.transpose(0, 2, 1).reshape(-1)
    lat_f = np.concatenate([cosine[:, arrive], sine[:, arrive]], 1)
    lat_i = np.concatenate([cosine[depart], sine[depart]], 1)
    freq = (y * nz + z).transpose(1, 0, 2).reshape(-1)
    core = a.transpose(1, 0, 2).reshape(-1)
    imag = -sine[:, freq]
    imag[:, freq == 0] = alternate[:, None]
    lon_i = np.concatenate(
        [
            np.concatenate([np.where(core == b, cosine[:, freq], 0.0), np.where(core == b, imag, 0.0)], 1)
            for b in (0, 1)
        ],
        0,
    )
    group = 2 * ny
    perm = np.zeros((n, n))
    for s in range(group):
        for t in range(nz):
            perm[t * group + s, s * nz + t] = 1.0
    pack = np.zeros((12 * nz, 16 * nz))
    for t in range(nz):
        for u in range(6):
            pack[t * 6 + u, t * 16 + u] = 1.0
            pack[6 * nz + t * 6 + u, t * 16 + 8 + u] = 1.0
    narrow = np.concatenate([*split_np(lon_f), perm.astype(jnp.bfloat16)], 0)
    wide = np.concatenate([*split_np(lat_f), *split_np(lat_i), *split_np(lon_i)], 0)
    return narrow, wide, pack.astype(jnp.bfloat16)


def split(values):
    high = values.astype(BF16)
    return high, (values - high.astype(F32)).astype(BF16)


def dot(left, right):
    return jnp.dot(left, right, preferred_element_type=F32)


def dot_t(left, right):
    return lax.dot_general(left, right, (((1,), (1,)), ((), ())), preferred_element_type=F32)


def dot_3(left, right, op=dot):
    return op(left[0], right[0]) + (op(left[1], right[0]) + op(left[0], right[1]))


def normalise(values):
    centred = values - jnp.mean(values, axis=-1, keepdims=True)
    inverse = lax.rsqrt(jnp.mean(centred * centred, axis=-1, keepdims=True) + NORM_EPSILON)
    return centred * inverse, inverse


def norm_linear(normed, inverse, values):
    along = jnp.mean(normed * values, axis=-1, keepdims=True)
    return inverse * (values - jnp.mean(values, axis=-1, keepdims=True) - normed * along)


def gelu_parts(values):
    cumulative = 0.5 * (1.0 + lax.erf(values * (1.0 / math.sqrt(2.0))))
    density = jnp.exp(-0.5 * values * values) * (1.0 / math.sqrt(2.0 * math.pi))
    return values * cumulative, cumulative + values * density


def swap_parts(values):
    return jnp.concatenate(
        [values[:, 128:256], values[:, 0:128], pltpu.roll(values[:, 256:384], 64, 1)], axis=1
    )


def kernel(
    ny,
    nz,
    nx,
    bg_ref,
    dir_ref,
    res_ref,
    spec_in_ref,
    spec_out_ref,
    mlp_in_ref,
    mlp_out_ref,
    readout_ref,
    owner_ref,
    cell_ref,
    count_ref,
    weight_ref,
    narrow_ref,
    wide_ref,
    pack_ref,
    grad_ref,
    scal_ref,
    s1,
    r1,
    s2,
    r2,
    wz,
    wblock,
    win,
    wout,
    slope_ref,
    mixes,
    arz,
    arc,
    arx,
    parts,
    sems,
    wsems,
    rsems,
):
    n = 2 * ny * nz
    chips = ny * nz
    group = 2 * ny
    lat = lax.axis_index("lat")
    ens = lax.axis_index("ens")
    core = lax.rem(lat, 2)
    chip = lax.div(lat, 2)
    yy = lax.div(chip, nz)
    zz = lax.rem(chip, nz)
    me_yc = yy * 2 + core

    def at_yc(k):
        return {"lat": (lax.div(k, 2) * nz + zz) * 2 + lax.rem(k, 2), "ens": ens}

    def at_z(t):
        return {"lat": (yy * nz + t) * 2 + core, "ens": ens}

    def at_x(t):
        return {"lat": lat, "ens": t}

    z_steps = sorted(range(1, nz), key=lambda s: (-min(s, nz - s), s))
    yc_partners = [lax.rem(me_yc + s, group) for s in range(1, group)]
    z_partners = [lax.rem(zz + s, nz) for s in z_steps]
    x_partners = [lax.rem(ens + s, nx) for s in range(1, nx)]
    y_partners = [lax.rem(yy + s, ny) for s in range(1, ny)]

    barrier = pltpu.get_barrier_semaphore()
    for k in yc_partners:
        pl.semaphore_signal(barrier, inc=1, device_id=at_yc(k), device_id_type=MESH)
    for t in z_partners:
        pl.semaphore_signal(barrier, inc=1, device_id=at_z(t), device_id_type=MESH)
    for t in x_partners:
        pl.semaphore_signal(barrier, inc=1, device_id=at_x(t), device_id_type=MESH)

    def push(source, target, send, recv, where):
        pltpu.make_async_remote_copy(
            src_ref=source,
            dst_ref=target,
            send_sem=send,
            recv_sem=recv,
            device_id=where,
            device_id_type=MESH,
        ).start()

    def arrive(ref, sem):
        pltpu.make_async_copy(ref, ref, sem).wait()

    def phase_one(f):
        for k in yc_partners:
            push(s1.at[f, k], r1.at[f, me_yc], sems.at[f, 0], sems.at[f, 1], at_yc(k))
        pltpu.make_async_copy(s1.at[f, me_yc], r1.at[f, me_yc], sems.at[f, 1]).start()

    def phase_two(f):
        arrive(r1.at[f], sems.at[f, 1])
        turned = dot(perm, r1[f].reshape(n, FEATURES))
        s2[f] = turned.reshape(nz, group, FEATURES).astype(BF16)
        for t in z_partners:
            push(s2.at[f, t], r2.at[f, zz], sems.at[f, 2], sems.at[f, 3], at_z(t))
        pltpu.make_async_copy(s2.at[f, zz], r2.at[f, zz], sems.at[f, 3]).start()

    def received(f):
        arrive(r2.at[f], sems.at[f, 3])
        return r2[f].astype(F32).reshape(n, FEATURES)

    lon_f = (narrow_ref[0:n, :], narrow_ref[n : 2 * n, :])
    perm = narrow_ref[2 * n : 3 * n, :]
    lat_f = (wide_ref[0:n, :], wide_ref[n : 2 * n, :])
    lat_i = (wide_ref[2 * n : 3 * n, :], wide_ref[3 * n : 4 * n, :])
    lon_i = (wide_ref[4 * n : 6 * n, :], wide_ref[6 * n : 8 * n, :])

    lane = lax.broadcasted_iota(jnp.int32, (1, FEATURES), 1)
    low_half = lax.rem(lane, 128) < 64
    tail_real = low_half == (core == 0)
    mask_r = jnp.where(jnp.logical_or(lane < 128, jnp.logical_and(lane >= 256, tail_real)), 1.0, 0.0)
    mask_i = 1.0 - mask_r
    plain = jnp.where(chip == 0, 0.0, 1.0)
    first = 1.0 - plain
    low_lane = lax.broadcasted_iota(jnp.int32, (1, 128), 1) < 64

    def lon_forward(f, field):
        spectrum = dot_3(lon_f, split(field))
        real, imag = spectrum[0:chips], spectrum[chips:n]
        imag_mid = pltpu.roll(imag[:, 128:256], 64, 1)
        real_mid = real[:, 128:256]
        for b in (0, 1):
            if b == 0:
                tiles = [real[:, 0:128], imag[:, 0:128], jnp.where(low_lane, real_mid, imag_mid)]
            else:
                tiles = [real[:, 256:384], imag[:, 256:384], jnp.where(low_lane, imag_mid, real_mid)]
            for i, tile in enumerate(tiles):
                low = tile.astype(BF16)
                for y in range(ny):
                    s1[f, 2 * y + b, :, i * 128 : (i + 1) * 128] = low[y * nz : (y + 1) * nz]

    def lon_inverse(f):
        values = received(f)
        tail = values[:, 256:384]
        stacked = jnp.concatenate(
            [
                jnp.concatenate([values[:, 0:128], tail], axis=1),
                jnp.concatenate([values[:, 128:256], pltpu.roll(tail, 64, 1)], axis=1),
            ],
            axis=0,
        ).astype(BF16)
        out = dot(lon_i[0], stacked) + dot(lon_i[1], stacked)
        middle_tile = jnp.where(low_lane, out[0:n, 128:256], out[n : 2 * n, 128:256])
        return jnp.concatenate([out[0:n, 0:128], middle_tile, out[n : 2 * n, 0:128]], axis=1)

    def lat_forward(f):
        x = received(f)
        sw = swap_parts(x)
        left = jnp.concatenate(
            [x * (mask_r + plain * mask_i), sw * (plain * mask_r - mask_i)], axis=0
        ).astype(BF16)
        right = jnp.concatenate(
            [
                x * (plain * mask_r - plain * mask_i) + sw * (first * mask_r),
                sw * (-plain) - x * (first * mask_i),
            ],
            axis=0,
        ).astype(BF16)
        return jnp.concatenate(
            [dot(lat_f[0], left) + dot(lat_f[1], left), dot(lat_f[0], right) + dot(lat_f[1], right)],
            axis=0,
        )

    def lat_inverse(f, both):
        a, b = both[0:n], both[n : 2 * n]
        sa, sb = swap_parts(a), swap_parts(b)
        upper = a * (mask_r + plain * mask_i) + b * (plain * (mask_r - mask_i)) + sb * (first * mask_i)
        lower = sa * (plain * mask_i - mask_r) - sb * plain - b * (first * mask_i)
        out = dot_3(lat_i, split(jnp.concatenate([upper, lower], axis=0)))
        s1[f] = out.reshape(group, nz, FEATURES).astype(BF16)

    def mix(values, which, op=dot):
        return dot_3(split(values), (mixes[2 * which], mixes[2 * which + 1]), op)

    state = bg_ref[...].astype(F32)
    heading = dir_ref[...]
    normed, inverse = normalise(state)
    lon_forward(0, normed)
    pick = lax.broadcasted_iota(jnp.int32, (16, 6), 0) - lax.broadcasted_iota(jnp.int32, (16, 6), 1)
    rows_in = dot_t(jnp.where(pick == 0, 1.0, 0.0).astype(BF16), mlp_in_ref[...])
    rows_out = dot(jnp.where(pick == 8, 1.0, 0.0).astype(BF16), mlp_out_ref[...])
    wblock[...] = (rows_in + rows_out).astype(BF16)

    pl.semaphore_wait(barrier, (group - 1) + (nz - 1) + (nx - 1))
    phase_one(0)
    for t in z_partners:
        push(wblock, wz.at[zz], wsems.at[0], wsems.at[1], at_z(t))
    pltpu.make_async_copy(wblock, wz.at[zz], wsems.at[1]).start()
    lon_forward(1, norm_linear(normed, inverse, heading))
    phase_one(1)
    phase_two(0)
    phase_two(1)

    rows = owner_ref.shape[0]
    owner_col = jnp.broadcast_to(owner_ref[...].astype(F32), (rows, rows))
    owner_row = owner_col.T
    cell_col = jnp.broadcast_to(cell_ref[...].astype(F32), (rows, rows)).T
    sub = lax.broadcasted_iota(jnp.int32, (rows, rows), 0)
    col = lax.broadcasted_iota(jnp.int32, (rows, rows), 1)
    again = jnp.where(jnp.logical_and(owner_col == owner_row, sub < col), 1.0, 0.0)
    rank = jnp.sum(again, axis=0, keepdims=True)
    slot = lax.broadcasted_iota(jnp.int32, (n, rows), 0)
    slot_k, slot_z = lax.div(slot, nz), lax.rem(slot, nz)
    slot_lat = (lax.div(slot_k, 2) * nz + slot_z) * 2 + lax.rem(slot_k, 2)
    mine = owner_row[0:1, :] == slot_lat.astype(F32)
    hit_a = jnp.where(jnp.logical_and(mine, rank == 0.0), 1.0, 0.0).astype(BF16)
    hit_b = jnp.where(jnp.logical_and(mine, rank == 1.0), 1.0, 0.0).astype(BF16)
    row_id = lax.broadcasted_iota(jnp.int32, weight_ref.shape, 0)
    weights = jnp.where(row_id < count_ref[...], weight_ref[...], 0.0).astype(BF16)
    cells = jnp.broadcast_to(cell_col[:, 0:1], (rows, 128)).astype(BF16)
    ids = jnp.where(low_lane, dot(hit_a, cells), dot(hit_b, cells))
    slots = jnp.concatenate([dot(hit_a, weights), dot(hit_b, weights), ids], axis=1)
    s1[2] = slots.reshape(group, nz, FEATURES).astype(BF16)
    phase_one(2)

    half = 4 * BLOCK
    p_row = lax.broadcasted_iota(jnp.int32, (FEATURES, 1), 0)

    def local_feature(p):
        within = lax.rem(p, 128)
        tail = lax.rem(p, 64)
        low_core = jnp.where(p < 256, within, 128 + tail)
        high_core = jnp.where(p < 256, 64 + within, tail)
        return jnp.where(core == 0, low_core, high_core)

    def block_of(u):
        return lax.div(u, BLOCK)

    row_tail_real = (lax.rem(p_row, 128) < 64) == (core == 0)
    row_real = jnp.logical_or(p_row < 128, jnp.logical_and(p_row >= 256, row_tail_real))
    u_row, u_lane = local_feature(p_row), local_feature(lane)
    spread = jnp.where(
        u_row == lax.broadcasted_iota(jnp.int32, (FEATURES, half), 1), 1.0, 0.0
    ).astype(BF16)
    widen = jnp.where(
        lax.broadcasted_iota(jnp.int32, (BLOCK, FEATURES), 0) == u_lane - BLOCK * block_of(u_lane), 1.0, 0.0
    ).astype(BF16)
    same_block = block_of(u_row) == block_of(u_lane)
    same_part = row_real == (mask_r > 0.5)
    cross_sign = jnp.where(row_real, 1.0, -1.0)
    for which, ref in ((0, spec_in_ref), (1, spec_out_ref)):
        real_pair = split(ref[0, pl.ds(core * half, half), :])
        imag_pair = split(ref[1, pl.ds(core * half, half), :])
        for level in (0, 1):
            real_part = dot(dot(spread, real_pair[level]).astype(BF16), widen)
            imag_part = dot(dot(spread, imag_pair[level]).astype(BF16), widen)
            dense = jnp.where(same_part, real_part, imag_part * cross_sign)
            mixes[2 * which + level] = jnp.where(same_block, dense, 0.0).astype(BF16)

    six = 6 * nz
    arrive(wz, wsems.at[1])
    packed = dot(pack_ref[...], wz[...].reshape(16 * nz, FEATURES)).astype(BF16)
    win[core, ens, yy] = packed[0:six]
    wout[core, ens, yy] = packed[six : 2 * six]
    for y in y_partners:
        push(win.at[core, ens, yy], win.at[core, ens, yy], wsems.at[2], wsems.at[3], at_yc(y * 2 + core))
    for t in x_partners:
        push(wout.at[core, ens, yy], wout.at[core, ens, yy], wsems.at[4], wsems.at[5], at_x(t))

    before = mix(lat_forward(0), 0)
    value, spec_slope = gelu_parts(before)
    lat_inverse(3, mix(value, 1))
    phase_one(3)

    sibling = at_yc(yy * 2 + (1 - core))
    arrive(win.at[0, 0, pl.ds(0, ny - 1)], wsems.at[3])
    for t in x_partners:
        push(win.at[core, ens], win.at[core, ens], wsems.at[6], wsems.at[7], at_x(t))
    push(win.at[core, ens], win.at[core, ens], wsems.at[10], wsems.at[11], sibling)
    arrive(wout.at[0, 0, pl.ds(0, nx - 1)], wsems.at[5])
    for y in y_partners:
        push(wout.at[core, :, yy], wout.at[core, :, yy], wsems.at[8], wsems.at[9], at_yc(y * 2 + core))
    push(wout.at[core, :, yy], wout.at[core, :, yy], wsems.at[12], wsems.at[13], sibling)

    lat_inverse(4, mix(spec_slope * mix(lat_forward(1), 0), 1))
    phase_one(4)
    phase_two(3)
    phase_two(2)
    phase_two(4)

    middle = state + lon_inverse(3)
    mixed, mixed_inverse = normalise(middle)
    mixed_low = mixed.astype(BF16)

    arrive(win.at[0, pl.ds(0, nx - 1)], wsems.at[7])
    for t in x_partners:
        push(win.at[core, t], win.at[core, t], wsems.at[10], wsems.at[11], sibling)
    arrive(wout.at[0, pl.ds(0, ny - 1)], wsems.at[9])
    for y in y_partners:
        push(wout.at[core, :, y], wout.at[core, :, y], wsems.at[12], wsems.at[13], sibling)

    got = received(2)
    cell_id = lax.broadcasted_iota(jnp.int32, (n, n), 1).astype(F32)
    at_a = jnp.where(got[:, 256:257] == cell_id, 1.0, 0.0)
    at_b = jnp.where(got[:, 320:321] == cell_id, 1.0, 0.0)
    cell_weights = dot(at_a.T.astype(BF16), got[:, 0:128].astype(BF16)) + dot(
        at_b.T.astype(BF16), got[:, 128:256].astype(BF16)
    )

    units = ny * six
    arrive(win.at[0], wsems.at[11])

    def slope_step(i, carry):
        block = win[lax.div(i, nx), lax.rem(i, nx)].reshape(units, FEATURES)
        slope_ref[i] = gelu_parts(dot_t(mixed_low, block))[1]
        return carry

    lax.fori_loop(0, 2 * nx, slope_step, 0)

    tangent_middle = heading + lon_inverse(4)
    tangent_low = norm_linear(mixed, mixed_inverse, tangent_middle).astype(BF16)
    arrive(wout.at[0], wsems.at[13])

    def tangent_step(i, total):
        co, t = lax.div(i, nx), lax.rem(i, nx)
        block_in = win[co, t].reshape(units, FEATURES)
        block_out = wout[co, t].reshape(units, FEATURES)
        hidden = (slope_ref[i] * dot_t(tangent_low, block_in)).astype(BF16)
        return total + dot(hidden, block_out)

    tangent_out = lax.fori_loop(0, 2 * nx, tangent_step, tangent_middle)

    readout = split(readout_ref[...])
    departures = dot_3(split(tangent_out), readout)
    gradient = dot_3(split(cell_weights * departures), readout, dot_t)
    gradient_low = gradient.astype(BF16)

    def grad_step(i, total):
        co, t = lax.div(i, nx), lax.rem(i, nx)
        block_in = win[co, t].reshape(units, FEATURES)
        block_out = wout[co, t].reshape(units, FEATURES)
        grad_pre = (slope_ref[i] * dot_t(gradient_low, block_out)).astype(BF16)
        return total + dot(grad_pre, block_in)

    grad_mixed = lax.fori_loop(0, 2 * nx, grad_step, jnp.zeros((n, FEATURES), F32))
    grad_middle = gradient + norm_linear(mixed, mixed_inverse, grad_mixed)

    lon_forward(5, grad_middle)
    phase_one(5)
    phase_two(5)
    lat_inverse(6, mix(spec_slope * mix(lat_forward(5), 1, dot_t), 0, dot_t))
    phase_one(6)
    phase_two(6)
    update = grad_middle + norm_linear(normed, inverse, lon_inverse(6))
    grad_ref[...] = update

    residual = res_ref[...]
    hessian = heading + update
    sums = [
        jnp.sum(jnp.sum(v, axis=0, keepdims=True), axis=1, keepdims=True)
        for v in (residual * residual, heading * hessian, residual * hessian, hessian * hessian)
    ]
    which = lax.broadcasted_iota(jnp.int32, (8, 128), 0)
    total = jnp.zeros((8, 128), F32)
    for i, value in enumerate(sums):
        total = total + jnp.where(which == i, value, 0.0)

    def reduce_over(i, total, buffer, mine_at, partners, where):
        parts[i] = total
        for t in partners:
            push(parts.at[i], buffer.at[mine_at], rsems.at[i, 0], rsems.at[i, 1], where(t))
        pltpu.make_async_copy(parts.at[i], buffer.at[mine_at], rsems.at[i, 1]).start()
        arrive(buffer, rsems.at[i, 1])
        return jnp.sum(buffer[...], axis=0)

    total = reduce_over(0, total, arz, zz, z_partners, at_z)
    total = reduce_over(1, total, arc, me_yc, yc_partners, at_yc)
    total = reduce_over(2, total, arx, ens, x_partners, at_x)
    norm_now, curvature, cross, square = total[0:1], total[1:2], total[2:3], total[3:4]
    step = norm_now / curvature
    norm_next = norm_now + step * (step * square - 2.0 * cross)
    ratio = norm_next / norm_now
    scal_ref[...] = jnp.where(which == 0, step, ratio)

    for f in range(FIELDS):
        arrive(s1.at[f, pl.ds(0, group - 1)], sems.at[f, 0])
        arrive(s2.at[f, pl.ds(0, nz - 1)], sems.at[f, 2])
    arrive(wz.at[pl.ds(0, nz - 1)], wsems.at[0])
    arrive(win.at[0, 0, pl.ds(0, ny - 1)], wsems.at[2])
    arrive(wout.at[0, 0, pl.ds(0, nx - 1)], wsems.at[4])
    arrive(win.at[0, pl.ds(0, nx - 1)], wsems.at[6])
    arrive(wout.at[0, pl.ds(0, ny - 1)], wsems.at[8])
    arrive(win.at[0], wsems.at[10])
    arrive(wout.at[0], wsems.at[12])
    arrive(arz.at[pl.ds(0, nz - 1)], rsems.at[0, 0])
    arrive(arc.at[pl.ds(0, group - 1)], rsems.at[1, 0])
    arrive(arx.at[pl.ds(0, nx - 1)], rsems.at[2, 0])


def per_device(ny, nz, nx, background, increment, residual, direction, spec_in, spec_out, mlp_in,
               mlp_out, readout, obs_owner, obs_cell, obs_count, obs_weight):
    n = background.shape[2]
    group = 2 * ny
    six = 6 * nz
    narrow, wide, pack = make_tables(ny, nz)
    vmem = pl.BlockSpec(memory_space=pltpu.VMEM)
    update, scal = pl.pallas_call(
        functools.partial(kernel, ny, nz, nx),
        out_shape=(
            jax.ShapeDtypeStruct((n, FEATURES), F32),
            jax.ShapeDtypeStruct((8, 128), F32),
        ),
        in_specs=[vmem] * 15,
        out_specs=(vmem, vmem),
        scratch_shapes=[
            pltpu.VMEM((FIELDS, group, nz, FEATURES), BF16),
            pltpu.VMEM((FIELDS, group, nz, FEATURES), BF16),
            pltpu.VMEM((FIELDS, nz, group, FEATURES), BF16),
            pltpu.VMEM((FIELDS, nz, group, FEATURES), BF16),
            pltpu.VMEM((nz, 16, FEATURES), BF16),
            pltpu.VMEM((16, FEATURES), BF16),
            pltpu.VMEM((2, nx, ny, six, FEATURES), BF16),
            pltpu.VMEM((2, nx, ny, six, FEATURES), BF16),
            pltpu.VMEM((2 * nx, n, ny * six), F32),
            pltpu.VMEM((4, FEATURES, FEATURES), BF16),
            pltpu.VMEM((nz, 8, 128), F32),
            pltpu.VMEM((group, 8, 128), F32),
            pltpu.VMEM((nx, 8, 128), F32),
            pltpu.VMEM((3, 8, 128), F32),
            pltpu.SemaphoreType.DMA((FIELDS, 4)),
            pltpu.SemaphoreType.DMA((14,)),
            pltpu.SemaphoreType.DMA((3, 2)),
        ],
        compiler_params=pltpu.CompilerParams(
            collective_id=0, has_side_effects=True, vmem_limit_bytes=48 * 1024 * 1024
        ),
    )(
        background.reshape(n, FEATURES),
        direction.reshape(n, FEATURES),
        residual.reshape(n, FEATURES),
        spec_in.reshape(2, FEATURES, BLOCK),
        spec_out.reshape(2, FEATURES, BLOCK),
        mlp_in,
        mlp_out,
        readout,
        obs_owner,
        obs_cell.reshape(1, -1),
        obs_count.reshape(1, 1),
        obs_weight,
        jnp.asarray(narrow),
        jnp.asarray(wide),
        jnp.asarray(pack),
    )
    step, ratio = scal[0, 0], scal[1, 0]
    hessian_dir = direction + update.reshape(direction.shape)
    residual_new = residual - step * hessian_dir
    return (
        increment + step * direction,
        residual_new,
        residual_new + ratio * direction,
        hessian_dir,
    )


def solution(mesh):
    n_lat, nx = mesh.shape["lat"], mesh.shape["ens"]
    nz = 16 if n_lat == 128 else 2
    ny = n_lat // (2 * nz)
    field = P("ens", "lat", None, None)
    return jax.shard_map(
        functools.partial(per_device, ny, nz, nx),
        mesh=mesh,
        in_specs=(
            field,
            field,
            field,
            field,
            P(),
            P(),
            P(None, ("lat", "ens")),
            P(("lat", "ens"), None),
            P(),
            P("lat", None),
            P("lat"),
            P("lat"),
            P("lat", None),
        ),
        out_specs=(field, field, field, field),
        check_vma=False,
    )
```

time: 793 us -> 122 us (0.15); the launches traced: 784 us -> 122 us
  waiting for transfers between devices: 343 us -> 0 us
  blocking collectives: 256 us -> 0 us
  Pallas kernels: 0 us -> 108 us
  starting transfers between devices: 69.5 us -> 0 us
  matrix products: 45.8 us -> 0 us
  local copies, waits for them, and re-layouts: 31.6 us -> 9.85 us
  other arithmetic: 19.6 us -> 2.17 us
  between operations: 18.8 us -> 1.4 us
    all_gather x2 -> x0, waiting for transfers between devices: 233 us -> none  [the longest x1 189 us: per_device(): lax.all_gather(mlp_out, ('lat', 'ens'), axis=0, tiled=True)]
    psum x2 -> x0, blocking collectives: 201 us -> none  [the longest x1 101 us: per_device(): norm_now = lax.psum(jnp.sum(residual * residual), ('lat', 'ens'))]
    all_to_all x7 -> x0, waiting for transfers between devices: 109 us -> none  [the longest x3 52.9 us: to_grid(): lax.all_to_all(field_pair.astype(jnp.bfloat16), 'lat', split_axis=1, conc...]
    pallas_call x0 -> x1, Pallas kernels: none -> 108 us  [per_device(): pl.pallas_call(functools.partial(kernel, ny, nz, nx), out_shape=(jax.Shap...]
    all_to_all x7 -> x0, starting transfers between devices: 69.5 us -> none  [the longest x3 21.4 us: to_grid(): lax.all_to_all(field_pair.astype(jnp.bfloat16), 'lat', split_axis=1, conc...]
    all_to_all x2 -> x0, blocking collectives: 54.8 us -> none  [the longest x1 28.8 us: per_device(): lax.all_to_all(outgoing.reshape(lat_groups, capacity, features).astype(jn...]
    dot_general x65 -> x0, matrix products: 45.8 us -> none  [the longest x2 6.4 us: contract(): return jnp.dot(left_rows, weight, preferred_element_type=jnp.float32)]
  transfers between devices with their start and end apart: 9 -> 0, of which waited for: 9 -> 0; matrix products, arithmetic and copies ran while one was open for 6% -> 0% of each run, Pallas kernels for 0% -> 0%
where the time goes in v1:
time: 122 us
  Pallas kernels  108 us (89%)
  local copies, waits for them, and re-layouts  9.85 us (8%)
  other arithmetic  2.17 us (2%)
  between operations  1.4 us (1%)
    pallas_call x1, Pallas kernels, per_device(): pl.pallas_call(functools.partial(kernel, ny, nz, nx), out_shape=(jax.Shap...  108 us
    unnamed x28, local copies, waits for them, and re-layouts  9.27 us

profile of v1, /device:TPU:1, one launch (start us, length us, event | category | flops | bytes accessed | tf_op | source)
XLA Modules:
  0.0 121.8 jit_solution(1917975159335999257)
XLA Ops:
  0.6 0.0 copy-start.6
  1.3 0.8 copy.21.owner_ref
  2.1 0.0 copy-start.9
  2.1 0.0 copy-start.10
  2.1 0.0 copy-start.11
  2.1 0.9 copy.20.mlp_in_ref
  3.0 0.0 copy-done.6
  3.0 0.0 copy-done.9
  3.0 0.0 copy-done.10
  3.0 0.0 copy-done.11
  3.0 0.0 copy-start
  3.1 0.9 copy-done
  4.0 0.0 copy-start.1
  4.0 0.9 copy-done.1
  4.9 0.0 copy-start.2
  4.9 1.0 copy-done.2
  5.9 0.0 copy-start.3
  5.9 1.0 copy-done.3
  6.9 0.0 copy-start.4
  6.9 1.0 copy-done.4
  7.9 0.0 copy-start.5
  7.9 0.9 copy-done.5
  8.9 0.0 copy-start.7
  8.9 0.9 copy-done.7
  9.8 0.0 copy-start.8
  9.8 0.9 copy-done.8
  10.7 0.0 copy-start.12
  10.7 108.4 %shard_map.183 = (f32[128,384]{1,0:T(8,128)S(1)}, f32[8,128]{1,0:T(8,128)S(1)}) custom-call(bf16[128,384]{1,0:T(8,128)(2,1)S(1)} %bitcast.17, f32[128,384]{1,0:T(8,128)S(1)} %bitcast.13, f32[128,384]{1,0:T(8,128)S(1)} %bitcast.14, f32[2,384,48]{2,1,0:T(8,128)S(1)} %bitcast.15, f32[2,384,48]{2,1,0:T(8,128)S(1)} %bitcast.16, ...), custom_call_target="tpu_custom_call" | custom-call | tf_op jit(solution)/shard_map/pallas_call | solution.py:507
  119.0 0.6 fusion
  119.6 0.0 copy-done.12
  119.6 2.2 %multiply_add_fusion = (f32[1,1,128,384]{3,2,1,0:T(8,128)}, f32[1,1,128,384]{3,2,1,0:T(8,128)}, f32[1,1,128,384]{3,2,1,0:T(8,128)}, f32[1,1,128,384]{3,2,1,0:T(8,128)}) fusion(f32[1,1,128,384]{3,2,1,0:T(8,128)S(1)} %copy-done, f32[]{:T(128)} %bitcast.9, f32[1,1,128,384]{3,2,1,0:T(8,128)S(1)} %copy-done.1, f32[]{:T(128)} %bitcast.7, ...), kind=kLoop, calls=%fused_computation.1 | loop fusion | flops 344064 | bytes 1572872 | tf_op jit(solution)/shard_map/add | solution.py:560
Async XLA Ops:
  0.6 2.4 %copy-start.6 = (bf16[1,1,128,384]{3,2,1,0:T(8,128)(2,1)S(1)}, bf16[1,1,128,384]{3,2,1,0:T(8,128)(2,1)}, u32[]{:S(2)}) copy-start(bf16[1,1,128,384]{3,2,1,0:T(8,128)(2,1)} %param.16) | copy-start | bytes 294916
  2.1 0.9 copy-start.9
  2.1 0.9 copy-start.10
  2.1 0.9 copy-start.11
  3.0 0.9 copy-start
  4.0 0.9 copy-start.1
  4.9 1.0 copy-start.2
  5.9 1.0 copy-start.3
  6.9 1.0 copy-start.4
  7.9 0.9 copy-start.5
  8.9 0.9 copy-start.7
  9.8 0.9 copy-start.8
  10.7 109.0 %copy-start.12 = (f32[1,1,128,384]{3,2,1,0:T(8,128)S(1)}, f32[1,1,128,384]{3,2,1,0:T(8,128)}, u32[]{:S(2)}) copy-start(f32[1,1,128,384]{3,2,1,0:T(8,128)} %param.17) | copy-start | bytes 589828

commit v2 on v1

--- a/solution.py
+++ b/solution.py
@@ -110,41 +110,45 @@
     ny,
     nz,
     nx,
-    bg_ref,
-    dir_ref,
-    res_ref,
-    spec_in_ref,
-    spec_out_ref,
-    mlp_in_ref,
-    mlp_out_ref,
-    readout_ref,
-    owner_ref,
-    cell_ref,
-    count_ref,
-    weight_ref,
-    narrow_ref,
-    wide_ref,
-    pack_ref,
-    grad_ref,
-    scal_ref,
-    s1,
-    r1,
-    s2,
-    r2,
-    wz,
-    wblock,
-    win,
-    wout,
-    slope_ref,
-    mixes,
-    arz,
-    arc,
-    arx,
-    parts,
-    sems,
-    wsems,
-    rsems,
+    *refs,
 ):
+    inputs, (grad_ref, scal_ref), held, rest = refs[:15], refs[15:17], refs[17:32], refs[32:]
+    (
+        bg_ref,
+        narrow_ref,
+        dir_ref,
+        mlp_in_ref,
+        mlp_out_ref,
+        wide_ref,
+        spec_in_ref,
+        spec_out_ref,
+        pack_ref,
+        owner_ref,
+        cell_ref,
+        count_ref,
+        weight_ref,
+        readout_ref,
+        res_ref,
+    ) = held
+    (
+        s1,
+        r1,
+        s2,
+        r2,
+        wz,
+        win,
+        wout,
+        slope_ref,
+        mixes,
+        around,
+        along,
+        parts,
+        sems,
+        zsems,
+        wsems,
+        rsems,
+        insems,
+    ) = rest
     n = 2 * ny * nz
     chips = ny * nz
     group = 2 * ny
@@ -168,16 +172,35 @@
     z_steps = sorted(range(1, nz), key=lambda s: (-min(s, nz - s), s))
     yc_partners = [lax.rem(me_yc + s, group) for s in range(1, group)]
     z_partners = [lax.rem(zz + s, nz) for s in z_steps]
-    x_partners = [lax.rem(ens + s, nx) for s in range(1, nx)]
-    y_partners = [lax.rem(yy + s, ny) for s in range(1, ny)]
-
+    plane = [
+        (lax.rem(me_yc + k, group), lax.rem(ens + t, nx))
+        for k, t in sorted(
+            ((k, t) for k in range(group) for t in range(nx) if k or t),
+            key=lambda p: -min(p[0] // 2, ny - p[0] // 2) - min(p[1], nx - p[1]),
+        )
+    ]
+
+    def at_plane(p):
+        return {"lat": (lax.div(p[0], 2) * nz + zz) * 2 + lax.rem(p[0], 2), "ens": p[1]}
+
+    for i in range(15):
+        pltpu.make_async_copy(inputs[i], held[i], insems.at[i]).start()
     barrier = pltpu.get_barrier_semaphore()
-    for k in yc_partners:
-        pl.semaphore_signal(barrier, inc=1, device_id=at_yc(k), device_id_type=MESH)
     for t in z_partners:
         pl.semaphore_signal(barrier, inc=1, device_id=at_z(t), device_id_type=MESH)
-    for t in x_partners:
-        pl.semaphore_signal(barrier, inc=1, device_id=at_x(t), device_id_type=MESH)
+    for p in plane:
+        pl.semaphore_signal(barrier, inc=1, device_id=at_plane(p), device_id_type=MESH)
+
+    ready = set()
+
+    def load(*wanted):
+        for ref in wanted:
+            i = next(k for k in range(15) if held[k] is ref)
+            if i not in ready:
+                ready.add(i)
+                pltpu.make_async_copy(inputs[i], ref, insems.at[i]).wait()
+
+    leaving, coming = [], {}
 
     def push(source, target, send, recv, where):
         pltpu.make_async_remote_copy(
@@ -189,31 +212,53 @@
             device_id_type=MESH,
         ).start()
 
-    def arrive(ref, sem):
+    def wait_bytes(ref, sem):
         pltpu.make_async_copy(ref, ref, sem).wait()
+
+    def arrive(key):
+        wait_bytes(*coming.pop(key))
+
+    def finish():
+        load(*held)
+        for key in list(coming):
+            arrive(key)
+        for ref, sem in leaving:
+            wait_bytes(ref, sem)
 
     def phase_one(f):
         for k in yc_partners:
             push(s1.at[f, k], r1.at[f, me_yc], sems.at[f, 0], sems.at[f, 1], at_yc(k))
         pltpu.make_async_copy(s1.at[f, me_yc], r1.at[f, me_yc], sems.at[f, 1]).start()
+        leaving.append((s1.at[f, pl.ds(0, group - 1)], sems.at[f, 0]))
+        coming["one", f] = (r1.at[f], sems.at[f, 1])
 
     def phase_two(f):
-        arrive(r1.at[f], sems.at[f, 1])
-        turned = dot(perm, r1[f].reshape(n, FEATURES))
+        arrive(("one", f))
+        turned = dot(narrow_ref[2 * n : 3 * n, :], r1[f].reshape(n, FEATURES))
         s2[f] = turned.reshape(nz, group, FEATURES).astype(BF16)
         for t in z_partners:
             push(s2.at[f, t], r2.at[f, zz], sems.at[f, 2], sems.at[f, 3], at_z(t))
         pltpu.make_async_copy(s2.at[f, zz], r2.at[f, zz], sems.at[f, 3]).start()
+        leaving.append((s2.at[f, pl.ds(0, nz - 1)], sems.at[f, 2]))
+        coming["two", f] = (r2.at[f], sems.at[f, 3])
 
     def received(f):
-        arrive(r2.at[f], sems.at[f, 3])
+        arrive(("two", f))
         return r2[f].astype(F32).reshape(n, FEATURES)
 
-    lon_f = (narrow_ref[0:n, :], narrow_ref[n : 2 * n, :])
-    perm = narrow_ref[2 * n : 3 * n, :]
-    lat_f = (wide_ref[0:n, :], wide_ref[n : 2 * n, :])
-    lat_i = (wide_ref[2 * n : 3 * n, :], wide_ref[3 * n : 4 * n, :])
-    lon_i = (wide_ref[4 * n : 6 * n, :], wide_ref[6 * n : 8 * n, :])
+    def lon_f():
+        load(narrow_ref)
+        return narrow_ref[0:n, :], narrow_ref[n : 2 * n, :]
+
+    def lat_f():
+        load(wide_ref)
+        return wide_ref[0:n, :], wide_ref[n : 2 * n, :]
+
+    def lat_i():
+        return wide_ref[2 * n : 3 * n, :], wide_ref[3 * n : 4 * n, :]
+
+    def lon_i():
+        return wide_ref[4 * n : 6 * n, :], wide_ref[6 * n : 8 * n, :]
 
     lane = lax.broadcasted_iota(jnp.int32, (1, FEATURES), 1)
     low_half = lax.rem(lane, 128) < 64
@@ -225,7 +270,7 @@
     low_lane = lax.broadcasted_iota(jnp.int32, (1, 128), 1) < 64
 
     def lon_forward(f, field):
-        spectrum = dot_3(lon_f, split(field))
+        spectrum = dot_3(lon_f(), split(field))
         real, imag = spectrum[0:chips], spectrum[chips:n]
         imag_mid = pltpu.roll(imag[:, 128:256], 64, 1)
         real_mid = real[:, 128:256]
@@ -249,11 +294,13 @@
             ],
             axis=0,
         ).astype(BF16)
-        out = dot(lon_i[0], stacked) + dot(lon_i[1], stacked)
+        high, low = lon_i()
+        out = dot(high, stacked) + dot(low, stacked)
         middle_tile = jnp.where(low_lane, out[0:n, 128:256], out[n : 2 * n, 128:256])
         return jnp.concatenate([out[0:n, 0:128], middle_tile, out[n : 2 * n, 0:128]], axis=1)
 
     def lat_forward(f):
+        high, low = lat_f()
         x = received(f)
         sw = swap_parts(x)
         left = jnp.concatenate(
@@ -267,7 +314,7 @@
             axis=0,
         ).astype(BF16)
         return jnp.concatenate(
-            [dot(lat_f[0], left) + dot(lat_f[1], left), dot(lat_f[0], right) + dot(lat_f[1], right)],
+            [dot(high, left) + dot(low, left), dot(high, right) + dot(low, right)],
             axis=0,
         )
 
@@ -276,34 +323,28 @@
         sa, sb = swap_parts(a), swap_parts(b)
         upper = a * (mask_r + plain * mask_i) + b * (plain * (mask_r - mask_i)) + sb * (first * mask_i)
         lower = sa * (plain * mask_i - mask_r) - sb * plain - b * (first * mask_i)
-        out = dot_3(lat_i, split(jnp.concatenate([upper, lower], axis=0)))
+        out = dot_3(lat_i(), split(jnp.concatenate([upper, lower], axis=0)))
         s1[f] = out.reshape(group, nz, FEATURES).astype(BF16)
 
     def mix(values, which, op=dot):
         return dot_3(split(values), (mixes[2 * which], mixes[2 * which + 1]), op)
 
+    load(bg_ref)
     state = bg_ref[...].astype(F32)
-    heading = dir_ref[...]
     normed, inverse = normalise(state)
     lon_forward(0, normed)
     pick = lax.broadcasted_iota(jnp.int32, (16, 6), 0) - lax.broadcasted_iota(jnp.int32, (16, 6), 1)
-    rows_in = dot_t(jnp.where(pick == 0, 1.0, 0.0).astype(BF16), mlp_in_ref[...])
+    load(mlp_in_ref, mlp_out_ref)
+    rows_in = dot(jnp.where(pick == 0, 1.0, 0.0).astype(BF16), mlp_in_ref[...])
     rows_out = dot(jnp.where(pick == 8, 1.0, 0.0).astype(BF16), mlp_out_ref[...])
-    wblock[...] = (rows_in + rows_out).astype(BF16)
-
-    pl.semaphore_wait(barrier, (group - 1) + (nz - 1) + (nx - 1))
-    phase_one(0)
-    for t in z_partners:
-        push(wblock, wz.at[zz], wsems.at[0], wsems.at[1], at_z(t))
-    pltpu.make_async_copy(wblock, wz.at[zz], wsems.at[1]).start()
+    wz[lax.rem(zz, min(4, nz)), lax.div(zz, min(4, nz))] = (rows_in + rows_out).astype(BF16)
+    load(dir_ref)
+    heading = dir_ref[...]
     lon_forward(1, norm_linear(normed, inverse, heading))
-    phase_one(1)
-    phase_two(0)
-    phase_two(1)
-
-    rows = owner_ref.shape[0]
-    owner_col = jnp.broadcast_to(owner_ref[...].astype(F32), (rows, rows))
-    owner_row = owner_col.T
+    load(owner_ref, cell_ref, count_ref, weight_ref)
+    rows = owner_ref.shape[1]
+    owner_row = jnp.broadcast_to(owner_ref[...].astype(F32), (rows, rows))
+    owner_col = owner_row.T
     cell_col = jnp.broadcast_to(cell_ref[...].astype(F32), (rows, rows)).T
     sub = lax.broadcasted_iota(jnp.int32, (rows, rows), 0)
     col = lax.broadcasted_iota(jnp.int32, (rows, rows), 1)
@@ -321,8 +362,31 @@
     ids = jnp.where(low_lane, dot(hit_a, cells), dot(hit_b, cells))
     slots = jnp.concatenate([dot(hit_a, weights), dot(hit_b, weights), ids], axis=1)
     s1[2] = slots.reshape(group, nz, FEATURES).astype(BF16)
+    pl.semaphore_wait(barrier, (nz - 1) + (group * nx - 1))
+    phase_one(0)
+    classes = min(4, nz)
+    quads = nz // classes
+    own_class, own_quad = lax.rem(zz, classes), lax.div(zz, classes)
+    far = sorted(range(1, quads), key=lambda q: -min(q, quads - q))
+    for q in far:
+        target = lax.rem(zz + classes * q, nz)
+        push(wz.at[own_class, own_quad], wz.at[own_class, own_quad], zsems.at[0], zsems.at[1], at_z(target))
+    if far:
+        leaving.append((wz.at[0, pl.ds(0, quads - 1)], zsems.at[0]))
+        coming["quads"] = (wz.at[0, pl.ds(0, quads - 1)], zsems.at[1])
+    phase_one(1)
     phase_one(2)
-
+    phase_two(0)
+    phase_two(1)
+    if far:
+        arrive("quads")
+    near = [1, nz - 1, 2][: classes - 1]
+    for step in near:
+        push(wz.at[own_class], wz.at[own_class], zsems.at[2], zsems.at[3], at_z(lax.rem(zz + step, nz)))
+    if near:
+        leaving.append((wz.at[pl.ds(0, classes - 1)], zsems.at[2]))
+        coming["classes"] = (wz.at[pl.ds(0, classes - 1)], zsems.at[3])
+    phase_two(2)
     half = 4 * BLOCK
     p_row = lax.broadcasted_iota(jnp.int32, (FEATURES, 1), 0)
 
@@ -348,6 +412,7 @@
     same_block = block_of(u_row) == block_of(u_lane)
     same_part = row_real == (mask_r > 0.5)
     cross_sign = jnp.where(row_real, 1.0, -1.0)
+    load(spec_in_ref, spec_out_ref)
     for which, ref in ((0, spec_in_ref), (1, spec_out_ref)):
         real_pair = split(ref[0, pl.ds(core * half, half), :])
         imag_pair = split(ref[1, pl.ds(core * half, half), :])
@@ -358,47 +423,110 @@
             mixes[2 * which + level] = jnp.where(same_block, dense, 0.0).astype(BF16)
 
     six = 6 * nz
-    arrive(wz, wsems.at[1])
+    sibling = at_yc(yy * 2 + (1 - core))
+
+    class Gather:
+        def __init__(self, ref, which, first, second, first_at, second_at, first_n, second_n):
+            self.ref, self.sem, self.f, self.g = ref, lambda i: wsems.at[which, i], first, second
+            self.first_at, self.second_at = first_at, second_at
+            self.nf, self.ng = first_n, second_n
+            self.left = lax.rem(second + second_n - 1, second_n)
+            self.right = lax.rem(second + 1, second_n)
+
+        def block(self, g, f):
+            return self.ref.at[core, g, f]
+
+        def offset(self, i):
+            return lax.rem(self.f + i, self.nf)
+
+        def beside(self, f):
+            mine = self.block(self.g, f)
+            if self.ng > 1:
+                push(mine, mine, self.sem(2), self.sem(3), self.second_at(self.right))
+            if self.ng > 2:
+                push(mine, mine, self.sem(4), self.sem(5), self.second_at(self.left))
+
+        def begin(self):
+            mine = self.block(self.g, self.f)
+            for i in range(1, self.nf):
+                push(mine, mine, self.sem(0), self.sem(1), self.first_at(self.offset(i)))
+            self.beside(self.f)
+            if self.nf > 1:
+                leaving.append((self.ref.at[0, 0, pl.ds(0, self.nf - 1)], self.sem(0)))
+                coming["first", self] = (self.ref.at[0, 0, pl.ds(0, self.nf - 1)], self.sem(1))
+            if self.ng > 1:
+                leaving.append((self.ref.at[0, 0], self.sem(2)))
+                coming["left", self] = (self.ref.at[0, 0], self.sem(3))
+            if self.ng > 2:
+                leaving.append((self.ref.at[0, 0], self.sem(4)))
+                coming["right", self] = (self.ref.at[0, 0], self.sem(5))
+
+        def cross(self, g, i):
+            slab = self.ref.at[core, g]
+            push(slab, slab, self.sem(8 + 2 * i), self.sem(9 + 2 * i), sibling)
+            leaving.append((slab, self.sem(8 + 2 * i)))
+            coming["core", self, i] = (slab, self.sem(9 + 2 * i))
+
+        def spread(self):
+            if self.nf > 1:
+                arrive(("first", self))
+            for i in range(1, self.nf):
+                self.beside(self.offset(i))
+
+        def cross_own(self):
+            self.cross(self.g, 0)
+
+        def pass_on(self):
+            for key in ("left", "right"):
+                if (key, self) in coming:
+                    arrive((key, self))
+            if self.ng > 2:
+                for i in range(self.nf):
+                    ref = self.block(self.left if i % 2 == 0 else self.right, self.offset(i))
+                    push(ref, ref, self.sem(6), self.sem(7), self.second_at(self.right if i % 2 == 0 else self.left))
+                leaving.append((self.ref.at[0, 0], self.sem(6)))
+                coming["opposite", self] = (self.ref.at[0, 0], self.sem(7))
+            if self.ng > 1:
+                self.cross(self.left, 1)
+            if self.ng > 2:
+                self.cross(self.right, 2)
+
+        def last(self):
+            if self.ng > 2:
+                arrive(("opposite", self))
+                self.cross(lax.rem(self.g + 2, self.ng), 3)
+
+        def slabs(self):
+            return [self.g, self.left, self.right, lax.rem(self.g + 2, self.ng)][: self.ng]
+
+    def at_y(t):
+        return at_yc(t * 2 + core)
+
+    gather_in = Gather(win, 0, yy, ens, at_y, at_x, ny, nx)
+    gather_out = Gather(wout, 1, ens, yy, at_x, at_y, nx, ny)
+    if near:
+        arrive("classes")
+    load(pack_ref)
     packed = dot(pack_ref[...], wz[...].reshape(16 * nz, FEATURES)).astype(BF16)
     win[core, ens, yy] = packed[0:six]
-    wout[core, ens, yy] = packed[six : 2 * six]
-    for y in y_partners:
-        push(win.at[core, ens, yy], win.at[core, ens, yy], wsems.at[2], wsems.at[3], at_yc(y * 2 + core))
-    for t in x_partners:
-        push(wout.at[core, ens, yy], wout.at[core, ens, yy], wsems.at[4], wsems.at[5], at_x(t))
-
+    wout[core, yy, ens] = packed[six : 2 * six]
+    gather_in.begin()
+    gather_out.begin()
     before = mix(lat_forward(0), 0)
     value, spec_slope = gelu_parts(before)
     lat_inverse(3, mix(value, 1))
     phase_one(3)
 
-    sibling = at_yc(yy * 2 + (1 - core))
-    arrive(win.at[0, 0, pl.ds(0, ny - 1)], wsems.at[3])
-    for t in x_partners:
-        push(win.at[core, ens], win.at[core, ens], wsems.at[6], wsems.at[7], at_x(t))
-    push(win.at[core, ens], win.at[core, ens], wsems.at[10], wsems.at[11], sibling)
-    arrive(wout.at[0, 0, pl.ds(0, nx - 1)], wsems.at[5])
-    for y in y_partners:
-        push(wout.at[core, :, yy], wout.at[core, :, yy], wsems.at[8], wsems.at[9], at_yc(y * 2 + core))
-    push(wout.at[core, :, yy], wout.at[core, :, yy], wsems.at[12], wsems.at[13], sibling)
-
     lat_inverse(4, mix(spec_slope * mix(lat_forward(1), 0), 1))
     phase_one(4)
+    gather_in.spread()
+    gather_out.spread()
     phase_two(3)
-    phase_two(2)
+    gather_in.cross_own()
+    gather_out.cross_own()
     phase_two(4)
-
-    middle = state + lon_inverse(3)
-    mixed, mixed_inverse = normalise(middle)
-    mixed_low = mixed.astype(BF16)
-
-    arrive(win.at[0, pl.ds(0, nx - 1)], wsems.at[7])
-    for t in x_partners:
-        push(win.at[core, t], win.at[core, t], wsems.at[10], wsems.at[11], sibling)
-    arrive(wout.at[0, pl.ds(0, ny - 1)], wsems.at[9])
-    for y in y_partners:
-        push(wout.at[core, :, y], wout.at[core, :, y], wsems.at[12], wsems.at[13], sibling)
-
+    gather_in.pass_on()
+    gather_out.pass_on()
     got = received(2)
     cell_id = lax.broadcasted_iota(jnp.int32, (n, n), 1).astype(F32)
     at_a = jnp.where(got[:, 256:257] == cell_id, 1.0, 0.0)
@@ -407,29 +535,38 @@
         at_b.T.astype(BF16), got[:, 128:256].astype(BF16)
     )
 
+    middle = state + lon_inverse(3)
+    mixed, mixed_inverse = normalise(middle)
+    mixed_low = mixed.astype(BF16)
+    gather_in.last()
+    gather_out.last()
+
     units = ny * six
-    arrive(win.at[0], wsems.at[11])
-
-    def slope_step(i, carry):
-        block = win[lax.div(i, nx), lax.rem(i, nx)].reshape(units, FEATURES)
-        slope_ref[i] = gelu_parts(dot_t(mixed_low, block))[1]
-        return carry
-
-    lax.fori_loop(0, 2 * nx, slope_step, 0)
-
+
+    def slope_of(co, g):
+        block = win[co, g].reshape(units, FEATURES)
+        slope_ref[co * nx + g] = gelu_parts(dot_t(mixed_low, block))[1]
+
+    for g in gather_in.slabs():
+        slope_of(core, g)
+    for i, g in enumerate(gather_in.slabs()):
+        arrive(("core", gather_in, i))
+        slope_of(1 - core, g)
     tangent_middle = heading + lon_inverse(4)
     tangent_low = norm_linear(mixed, mixed_inverse, tangent_middle).astype(BF16)
-    arrive(wout.at[0], wsems.at[13])
+    for i in range(ny):
+        arrive(("core", gather_out, i))
 
     def tangent_step(i, total):
         co, t = lax.div(i, nx), lax.rem(i, nx)
         block_in = win[co, t].reshape(units, FEATURES)
-        block_out = wout[co, t].reshape(units, FEATURES)
+        block_out = wout[co, :, t].reshape(units, FEATURES)
         hidden = (slope_ref[i] * dot_t(tangent_low, block_in)).astype(BF16)
         return total + dot(hidden, block_out)
 
     tangent_out = lax.fori_loop(0, 2 * nx, tangent_step, tangent_middle)
 
+    load(readout_ref)
     readout = split(readout_ref[...])
     departures = dot_3(split(tangent_out), readout)
     gradient = dot_3(split(cell_weights * departures), readout, dot_t)
@@ -438,7 +575,7 @@
     def grad_step(i, total):
         co, t = lax.div(i, nx), lax.rem(i, nx)
         block_in = win[co, t].reshape(units, FEATURES)
-        block_out = wout[co, t].reshape(units, FEATURES)
+        block_out = wout[co, :, t].reshape(units, FEATURES)
         grad_pre = (slope_ref[i] * dot_t(gradient_low, block_out)).astype(BF16)
         return total + dot(grad_pre, block_in)
 
@@ -454,47 +591,36 @@
     update = grad_middle + norm_linear(normed, inverse, lon_inverse(6))
     grad_ref[...] = update
 
+    load(res_ref)
     residual = res_ref[...]
     hessian = heading + update
     sums = [
         jnp.sum(jnp.sum(v, axis=0, keepdims=True), axis=1, keepdims=True)
         for v in (residual * residual, heading * hessian, residual * hessian, hessian * hessian)
     ]
-    which = lax.broadcasted_iota(jnp.int32, (8, 128), 0)
-    total = jnp.zeros((8, 128), F32)
+    place = lax.broadcasted_iota(jnp.int32, (1, 128), 1)
+    total = jnp.zeros((1, 128), F32)
     for i, value in enumerate(sums):
-        total = total + jnp.where(which == i, value, 0.0)
+        total = total + jnp.where(place == i, value, 0.0)
 
     def reduce_over(i, total, buffer, mine_at, partners, where):
         parts[i] = total
         for t in partners:
             push(parts.at[i], buffer.at[mine_at], rsems.at[i, 0], rsems.at[i, 1], where(t))
         pltpu.make_async_copy(parts.at[i], buffer.at[mine_at], rsems.at[i, 1]).start()
-        arrive(buffer, rsems.at[i, 1])
+        leaving.append((buffer.at[pl.ds(0, len(partners))], rsems.at[i, 0]))
+        wait_bytes(buffer, rsems.at[i, 1])
         return jnp.sum(buffer[...], axis=0)
 
-    total = reduce_over(0, total, arz, zz, z_partners, at_z)
-    total = reduce_over(1, total, arc, me_yc, yc_partners, at_yc)
-    total = reduce_over(2, total, arx, ens, x_partners, at_x)
-    norm_now, curvature, cross, square = total[0:1], total[1:2], total[2:3], total[3:4]
+    total = reduce_over(0, total, around, me_yc * nx + ens, plane, at_plane)
+    total = reduce_over(1, total, along, zz, z_partners, at_z)
+    norm_now, curvature, cross, square = total[:, 0:1], total[:, 1:2], total[:, 2:3], total[:, 3:4]
     step = norm_now / curvature
     norm_next = norm_now + step * (step * square - 2.0 * cross)
     ratio = norm_next / norm_now
-    scal_ref[...] = jnp.where(which == 0, step, ratio)
-
-    for f in range(FIELDS):
-        arrive(s1.at[f, pl.ds(0, group - 1)], sems.at[f, 0])
-        arrive(s2.at[f, pl.ds(0, nz - 1)], sems.at[f, 2])
-    arrive(wz.at[pl.ds(0, nz - 1)], wsems.at[0])
-    arrive(win.at[0, 0, pl.ds(0, ny - 1)], wsems.at[2])
-    arrive(wout.at[0, 0, pl.ds(0, nx - 1)], wsems.at[4])
-    arrive(win.at[0, pl.ds(0, nx - 1)], wsems.at[6])
-    arrive(wout.at[0, pl.ds(0, ny - 1)], wsems.at[8])
-    arrive(win.at[0], wsems.at[10])
-    arrive(wout.at[0], wsems.at[12])
-    arrive(arz.at[pl.ds(0, nz - 1)], rsems.at[0, 0])
-    arrive(arc.at[pl.ds(0, group - 1)], rsems.at[1, 0])
-    arrive(arx.at[pl.ds(0, nx - 1)], rsems.at[2, 0])
+    line = lax.broadcasted_iota(jnp.int32, (8, FEATURES), 0)
+    scal_ref[...] = jnp.where(line == 0, step, ratio)
+    finish()
 
 
 def per_device(ny, nz, nx, background, increment, residual, direction, spec_in, spec_out, mlp_in,
@@ -504,54 +630,56 @@
     six = 6 * nz
     narrow, wide, pack = make_tables(ny, nz)
     vmem = pl.BlockSpec(memory_space=pltpu.VMEM)
+    operands = (
+        background.reshape(n, FEATURES),
+        jnp.asarray(narrow),
+        direction.reshape(n, FEATURES),
+        mlp_in.T,
+        mlp_out,
+        jnp.asarray(wide),
+        spec_in.reshape(2, FEATURES, BLOCK),
+        spec_out.reshape(2, FEATURES, BLOCK),
+        jnp.asarray(pack),
+        obs_owner.reshape(1, -1),
+        obs_cell.reshape(1, -1),
+        obs_count.reshape(1, 1),
+        obs_weight,
+        readout,
+        residual.reshape(n, FEATURES),
+    )
     update, scal = pl.pallas_call(
         functools.partial(kernel, ny, nz, nx),
         out_shape=(
             jax.ShapeDtypeStruct((n, FEATURES), F32),
-            jax.ShapeDtypeStruct((8, 128), F32),
+            jax.ShapeDtypeStruct((8, FEATURES), F32),
         ),
-        in_specs=[vmem] * 15,
+        in_specs=[pl.BlockSpec(memory_space=pl.ANY)] * 15,
         out_specs=(vmem, vmem),
-        scratch_shapes=[
+        scratch_shapes=[pltpu.VMEM(v.shape, v.dtype) for v in operands]
+        + [
             pltpu.VMEM((FIELDS, group, nz, FEATURES), BF16),
             pltpu.VMEM((FIELDS, group, nz, FEATURES), BF16),
             pltpu.VMEM((FIELDS, nz, group, FEATURES), BF16),
             pltpu.VMEM((FIELDS, nz, group, FEATURES), BF16),
-            pltpu.VMEM((nz, 16, FEATURES), BF16),
-            pltpu.VMEM((16, FEATURES), BF16),
+            pltpu.VMEM((min(4, nz), nz // min(4, nz), 16, FEATURES), BF16),
             pltpu.VMEM((2, nx, ny, six, FEATURES), BF16),
-            pltpu.VMEM((2, nx, ny, six, FEATURES), BF16),
+            pltpu.VMEM((2, ny, nx, six, FEATURES), BF16),
             pltpu.VMEM((2 * nx, n, ny * six), F32),
             pltpu.VMEM((4, FEATURES, FEATURES), BF16),
-            pltpu.VMEM((nz, 8, 128), F32),
-            pltpu.VMEM((group, 8, 128), F32),
-            pltpu.VMEM((nx, 8, 128), F32),
-            pltpu.VMEM((3, 8, 128), F32),
+            pltpu.VMEM((group * nx, 1, 128), F32),
+            pltpu.VMEM((nz, 1, 128), F32),
+            pltpu.VMEM((2, 1, 128), F32),
             pltpu.SemaphoreType.DMA((FIELDS, 4)),
-            pltpu.SemaphoreType.DMA((14,)),
-            pltpu.SemaphoreType.DMA((3, 2)),
+            pltpu.SemaphoreType.DMA((4,)),
+            pltpu.SemaphoreType.DMA((2, 16)),
+            pltpu.SemaphoreType.DMA((2, 2)),
+            pltpu.SemaphoreType.DMA((15,)),
         ],
         compiler_params=pltpu.CompilerParams(
             collective_id=0, has_side_effects=True, vmem_limit_bytes=48 * 1024 * 1024
         ),
-    )(
-        background.reshape(n, FEATURES),
-        direction.reshape(n, FEATURES),
-        residual.reshape(n, FEATURES),
-        spec_in.reshape(2, FEATURES, BLOCK),
-        spec_out.reshape(2, FEATURES, BLOCK),
-        mlp_in,
-        mlp_out,
-        readout,
-        obs_owner,
-        obs_cell.reshape(1, -1),
-        obs_count.reshape(1, 1),
-        obs_weight,
-        jnp.asarray(narrow),
-        jnp.asarray(wide),
-        jnp.asarray(pack),
-    )
-    step, ratio = scal[0, 0], scal[1, 0]
+    )(*operands)
+    step, ratio = scal[0:1], scal[1:2]
     hessian_dir = direction + update.reshape(direction.shape)
     residual_new = residual - step * hessian_dir
     return (

time: 122 us -> 121 us (level)
  other arithmetic: 2.17 us -> 0.93 us
    add x1, other arithmetic: 2.17 us -> 0.93 us  [per_device(): residual_new + ratio * direction]
    unnamed x28 -> x30, local copies, waits for them, and re-layouts: 9.27 us -> 10 us
where the time goes in v2:
time: 121 us; the launch traced here: 120 us
  Pallas kernels  108 us (89%)
  local copies, waits for them, and re-layouts  10 us (8%)
  between operations  1.34 us (1%)
    pallas_call x1, Pallas kernels, per_device(): pl.pallas_call(functools.partial(kernel, ny, nz, nx), out_shape=(jax.Shap...  108 us
    unnamed x30, local copies, waits for them, and re-layouts  10 us

profile of v2, /device:TPU:1, one launch (start us, length us, event | category | flops | bytes accessed | tf_op | source)
XLA Modules:
  0.0 120.5 jit_solution(1843248892855539404)
XLA Ops:
  1.3 0.0 copy-start.11
  1.3 0.0 copy-start.10
  1.3 0.0 copy-start.12
  1.3 0.0 copy-start.13
  1.3 0.7 copy-done.11
  2.0 0.0 copy-done.10
  2.0 0.0 copy-done.12
  2.0 0.0 copy-done.13
  2.0 0.0 copy-start
  2.0 0.9 copy-done
  2.9 0.0 copy-start.1
  2.9 0.9 copy-done.1
  3.9 0.0 copy-start.2
  3.9 1.0 copy-done.2
  4.9 0.0 copy-start.3
  4.9 1.0 copy-done.3
  5.9 0.0 copy-start.4
  5.9 1.0 copy-done.4
  6.9 0.0 copy-start.5
  6.9 0.9 copy-done.5
  7.8 0.0 copy-start.6
  7.8 0.9 copy-done.6
  8.7 0.0 copy-start.7
  8.7 0.9 copy-done.7
  9.6 0.0 copy-start.8
  9.6 0.9 copy-done.8
  10.5 0.0 copy-start.9
  10.5 0.8 copy-done.9
  11.3 0.0 copy-start.14
  11.3 108.2 %shard_map.183 = (f32[128,384]{1,0:T(8,128)S(1)}, f32[8,384]{1,0:T(8,128)S(1)}) custom-call(bf16[128,384]{1,0:T(8,128)(2,1)S(1)} %bitcast.17, bf16[384,128]{1,0:T(8,128)(2,1)S(1)} %copy-done.8, f32[128,384]{1,0:T(8,128)S(1)} %bitcast.13, bf16[6,384]{1,0:T(8,128)(2,1)S(1)} %bitcast.18, bf16[6,384]{1,0:T(8,128)(2,1)S(1)} %copy-done.11, ...), custom_call_target="tpu_custom_call" | custom-call | tf_op jit(solution)/shard_map/pallas_call | solution.py:650
  119.5 0.0 copy-done.14
  119.6 0.9 multiply_add_fusion
  (1 shorter events, 0.0 us)
Async XLA Ops:
  1.3 0.7 copy-start.11
  1.3 0.7 copy-start.10
  1.3 0.7 copy-start.12
  1.3 0.7 copy-start.13
  2.0 0.9 copy-start
  2.9 0.9 copy-start.1
  3.9 1.0 copy-start.2
  4.9 1.0 copy-start.3
  5.9 1.0 copy-start.4
  6.9 0.9 copy-start.5
  7.8 0.9 copy-start.6
  8.7 0.9 copy-start.7
  9.6 0.9 copy-start.8
  10.5 0.8 copy-start.9
  11.3 108.2 %copy-start.14 = (f32[1,1,128,384]{3,2,1,0:T(8,128)S(1)}, f32[1,1,128,384]{3,2,1,0:T(8,128)}, u32[]{:S(2)}) copy-start(f32[1,1,128,384]{3,2,1,0:T(8,128)} %param.17) | copy-start | bytes 589828

commit v3 on v2

--- a/solution.py
+++ b/solution.py
@@ -16,6 +16,7 @@
 FEATURES = 384
 BLOCK = 48
 FIELDS = 7
+VMEM_BYTES = 63 * 1024 * 1024
 
 
 def split_np(table):
@@ -112,7 +113,7 @@
     nx,
     *refs,
 ):
-    inputs, (grad_ref, scal_ref), held, rest = refs[:15], refs[15:17], refs[17:32], refs[32:]
+    inputs, (grad_ref, step_ref, ratio_ref), held, rest = refs[:15], refs[15:18], refs[18:33], refs[33:]
     (
         bg_ref,
         narrow_ref,
@@ -139,6 +140,7 @@
         win,
         wout,
         slope_ref,
+        hidden,
         mixes,
         around,
         along,
@@ -377,16 +379,6 @@
     phase_one(1)
     phase_one(2)
     phase_two(0)
-    phase_two(1)
-    if far:
-        arrive("quads")
-    near = [1, nz - 1, 2][: classes - 1]
-    for step in near:
-        push(wz.at[own_class], wz.at[own_class], zsems.at[2], zsems.at[3], at_z(lax.rem(zz + step, nz)))
-    if near:
-        leaving.append((wz.at[pl.ds(0, classes - 1)], zsems.at[2]))
-        coming["classes"] = (wz.at[pl.ds(0, classes - 1)], zsems.at[3])
-    phase_two(2)
     half = 4 * BLOCK
     p_row = lax.broadcasted_iota(jnp.int32, (FEATURES, 1), 0)
 
@@ -422,74 +414,91 @@
             dense = jnp.where(same_part, real_part, imag_part * cross_sign)
             mixes[2 * which + level] = jnp.where(same_block, dense, 0.0).astype(BF16)
 
+    if far:
+        arrive("quads")
+    near = [1, nz - 1, 2][: classes - 1]
+    for step in near:
+        push(wz.at[own_class], wz.at[own_class], zsems.at[2], zsems.at[3], at_z(lax.rem(zz + step, nz)))
+    if near:
+        leaving.append((wz.at[pl.ds(0, classes - 1)], zsems.at[2]))
+        coming["classes"] = (wz.at[pl.ds(0, classes - 1)], zsems.at[3])
+    phase_two(1)
     six = 6 * nz
     sibling = at_yc(yy * 2 + (1 - core))
 
     class Gather:
         def __init__(self, ref, which, first, second, first_at, second_at, first_n, second_n):
             self.ref, self.sem, self.f, self.g = ref, lambda i: wsems.at[which, i], first, second
-            self.first_at, self.second_at = first_at, second_at
+            self.which, self.first_at, self.second_at = which, first_at, second_at
             self.nf, self.ng = first_n, second_n
             self.left = lax.rem(second + second_n - 1, second_n)
             self.right = lax.rem(second + 1, second_n)
+            self.order = sorted(range(first_n), key=lambda i: (min(i, first_n - i), i))
 
         def block(self, g, f):
-            return self.ref.at[core, g, f]
+            return self.ref.at[core, g, f] if self.which == 0 else self.ref.at[core, f, g]
+
+        def slab(self, g):
+            return self.ref.at[core, g] if self.which == 0 else self.ref.at[core, :, g]
+
+        def blocks(self, count):
+            part = pl.ds(0, count)
+            return self.ref.at[0, 0, part] if self.which == 0 else self.ref.at[0, part, 0]
 
         def offset(self, i):
             return lax.rem(self.f + i, self.nf)
 
-        def beside(self, f):
-            mine = self.block(self.g, f)
+        def beside(self, i):
+            mine = self.block(self.g, self.offset(i))
             if self.ng > 1:
-                push(mine, mine, self.sem(2), self.sem(3), self.second_at(self.right))
+                push(mine, mine, self.sem(4), self.sem(8 + i), self.second_at(self.right))
+                coming["left", self, i] = (self.blocks(1), self.sem(8 + i))
             if self.ng > 2:
-                push(mine, mine, self.sem(4), self.sem(5), self.second_at(self.left))
+                push(mine, mine, self.sem(5), self.sem(12 + i), self.second_at(self.left))
+                coming["right", self, i] = (self.blocks(1), self.sem(12 + i))
 
         def begin(self):
             mine = self.block(self.g, self.f)
-            for i in range(1, self.nf):
-                push(mine, mine, self.sem(0), self.sem(1), self.first_at(self.offset(i)))
-            self.beside(self.f)
+            for i in self.order[1:]:
+                push(mine, mine, self.sem(0), self.sem(self.nf - i), self.first_at(self.offset(i)))
+                coming["first", self, self.nf - i] = (self.blocks(1), self.sem(self.nf - i))
+            self.beside(0)
             if self.nf > 1:
-                leaving.append((self.ref.at[0, 0, pl.ds(0, self.nf - 1)], self.sem(0)))
-                coming["first", self] = (self.ref.at[0, 0, pl.ds(0, self.nf - 1)], self.sem(1))
+                leaving.append((self.blocks(self.nf - 1), self.sem(0)))
             if self.ng > 1:
-                leaving.append((self.ref.at[0, 0], self.sem(2)))
-                coming["left", self] = (self.ref.at[0, 0], self.sem(3))
+                leaving.append((self.blocks(self.nf), self.sem(4)))
             if self.ng > 2:
-                leaving.append((self.ref.at[0, 0], self.sem(4)))
-                coming["right", self] = (self.ref.at[0, 0], self.sem(5))
+                leaving.append((self.blocks(self.nf), self.sem(5)))
+
+        def spread(self, i):
+            arrive(("first", self, i))
+            self.beside(i)
 
         def cross(self, g, i):
-            slab = self.ref.at[core, g]
-            push(slab, slab, self.sem(8 + 2 * i), self.sem(9 + 2 * i), sibling)
-            leaving.append((slab, self.sem(8 + 2 * i)))
-            coming["core", self, i] = (slab, self.sem(9 + 2 * i))
-
-        def spread(self):
-            if self.nf > 1:
-                arrive(("first", self))
-            for i in range(1, self.nf):
-                self.beside(self.offset(i))
-
-        def cross_own(self):
-            self.cross(self.g, 0)
-
-        def pass_on(self):
-            for key in ("left", "right"):
-                if (key, self) in coming:
-                    arrive((key, self))
-            if self.ng > 2:
-                for i in range(self.nf):
-                    ref = self.block(self.left if i % 2 == 0 else self.right, self.offset(i))
-                    push(ref, ref, self.sem(6), self.sem(7), self.second_at(self.right if i % 2 == 0 else self.left))
-                leaving.append((self.ref.at[0, 0], self.sem(6)))
-                coming["opposite", self] = (self.ref.at[0, 0], self.sem(7))
-            if self.ng > 1:
-                self.cross(self.left, 1)
-            if self.ng > 2:
-                self.cross(self.right, 2)
+            slab = self.slab(g)
+            push(slab, slab, self.sem(16 + 2 * i), self.sem(17 + 2 * i), sibling)
+            leaving.append((slab, self.sem(16 + 2 * i)))
+            coming["core", self, i] = (slab, self.sem(17 + 2 * i))
+
+        def pass_on(self, i):
+            half = six // 2
+            for key, origin, target, part in (
+                ("left", self.left, self.right, pl.ds(0, half)),
+                ("right", self.right, self.left, pl.ds(half, half)),
+            ):
+                if (key, self, i) in coming:
+                    arrive((key, self, i))
+                if self.ng > 2:
+                    ref = self.block(origin, self.offset(i)).at[part]
+                    push(ref, ref, self.sem(6), self.sem(7), self.second_at(target))
+            if i == self.order[-1]:
+                if self.ng > 2:
+                    leaving.append((self.blocks(self.nf), self.sem(6)))
+                    coming["opposite", self] = (self.blocks(self.nf), self.sem(7))
+                if self.ng > 1:
+                    self.cross(self.left, 1)
+                if self.ng > 2:
+                    self.cross(self.right, 2)
 
         def last(self):
             if self.ng > 2:
@@ -504,29 +513,51 @@
 
     gather_in = Gather(win, 0, yy, ens, at_y, at_x, ny, nx)
     gather_out = Gather(wout, 1, ens, yy, at_x, at_y, nx, ny)
+    before = mix(lat_forward(0), 0)
+    value, spec_slope = gelu_parts(before)
+    lat_inverse(3, mix(value, 1))
+    phase_one(3)
     if near:
         arrive("classes")
     load(pack_ref)
     packed = dot(pack_ref[...], wz[...].reshape(16 * nz, FEATURES)).astype(BF16)
     win[core, ens, yy] = packed[0:six]
-    wout[core, yy, ens] = packed[six : 2 * six]
+    wout[core, ens, yy] = packed[six : 2 * six]
     gather_in.begin()
     gather_out.begin()
-    before = mix(lat_forward(0), 0)
-    value, spec_slope = gelu_parts(before)
-    lat_inverse(3, mix(value, 1))
-    phase_one(3)
+    phase_two(3)
 
     lat_inverse(4, mix(spec_slope * mix(lat_forward(1), 0), 1))
     phase_one(4)
-    gather_in.spread()
-    gather_out.spread()
-    phase_two(3)
-    gather_in.cross_own()
-    gather_out.cross_own()
+    for i in range(1, max(nx, ny)):
+        for gather in (gather_in, gather_out):
+            if i < gather.nf:
+                gather.spread(gather.order[i])
     phase_two(4)
-    gather_in.pass_on()
-    gather_out.pass_on()
+    for gather in (gather_in, gather_out):
+        gather.cross(gather.g, 0)
+    phase_two(2)
+    for i in range(max(nx, ny)):
+        for gather in (gather_in, gather_out):
+            if i < gather.nf:
+                gather.pass_on(gather.order[i])
+
+    middle = state + lon_inverse(3)
+    mixed, mixed_inverse = normalise(middle)
+    mixed_low = mixed.astype(BF16)
+
+    units = ny * six
+
+    def slope_of(co, g):
+        block = win[co, g].reshape(units, FEATURES)
+        slope_ref[co * nx + g] = gelu_parts(dot_t(mixed_low, block))[1]
+
+    slabs = gather_in.slabs()
+    slope_of(core, slabs[0])
+    arrive(("core", gather_in, 0))
+    slope_of(1 - core, slabs[0])
+    for i in range(1, min(3, nx)):
+        slope_of(core, slabs[i])
     got = received(2)
     cell_id = lax.broadcasted_iota(jnp.int32, (n, n), 1).astype(F32)
     at_a = jnp.where(got[:, 256:257] == cell_id, 1.0, 0.0)
@@ -535,51 +566,32 @@
         at_b.T.astype(BF16), got[:, 128:256].astype(BF16)
     )
 
-    middle = state + lon_inverse(3)
-    mixed, mixed_inverse = normalise(middle)
-    mixed_low = mixed.astype(BF16)
     gather_in.last()
     gather_out.last()
-
-    units = ny * six
-
-    def slope_of(co, g):
-        block = win[co, g].reshape(units, FEATURES)
-        slope_ref[co * nx + g] = gelu_parts(dot_t(mixed_low, block))[1]
-
-    for g in gather_in.slabs():
-        slope_of(core, g)
-    for i, g in enumerate(gather_in.slabs()):
+    for i in range(1, nx):
+        if i == 3:
+            slope_of(core, slabs[i])
         arrive(("core", gather_in, i))
-        slope_of(1 - core, g)
+        slope_of(1 - core, slabs[i])
     tangent_middle = heading + lon_inverse(4)
     tangent_low = norm_linear(mixed, mixed_inverse, tangent_middle).astype(BF16)
     for i in range(ny):
         arrive(("core", gather_out, i))
 
-    def tangent_step(i, total):
-        co, t = lax.div(i, nx), lax.rem(i, nx)
-        block_in = win[co, t].reshape(units, FEATURES)
-        block_out = wout[co, :, t].reshape(units, FEATURES)
-        hidden = (slope_ref[i] * dot_t(tangent_low, block_in)).astype(BF16)
-        return total + dot(hidden, block_out)
-
-    tangent_out = lax.fori_loop(0, 2 * nx, tangent_step, tangent_middle)
-
+    def through(values_low, ref):
+        for i in range(2 * nx):
+            block = ref[i // nx, i % nx].reshape(units, FEATURES)
+            hidden[:, i * units : (i + 1) * units] = (slope_ref[i] * dot_t(values_low, block)).astype(BF16)
+        return hidden[...]
+
+    tangent_out = tangent_middle + dot(through(tangent_low, win), wout[...].reshape(-1, FEATURES))
     load(readout_ref)
     readout = split(readout_ref[...])
     departures = dot_3(split(tangent_out), readout)
     gradient = dot_3(split(cell_weights * departures), readout, dot_t)
     gradient_low = gradient.astype(BF16)
 
-    def grad_step(i, total):
-        co, t = lax.div(i, nx), lax.rem(i, nx)
-        block_in = win[co, t].reshape(units, FEATURES)
-        block_out = wout[co, :, t].reshape(units, FEATURES)
-        grad_pre = (slope_ref[i] * dot_t(gradient_low, block_out)).astype(BF16)
-        return total + dot(grad_pre, block_in)
-
-    grad_mixed = lax.fori_loop(0, 2 * nx, grad_step, jnp.zeros((n, FEATURES), F32))
+    grad_mixed = dot(through(gradient_low, wout), win[...].reshape(-1, FEATURES))
     grad_middle = gradient + norm_linear(mixed, mixed_inverse, grad_mixed)
 
     lon_forward(5, grad_middle)
@@ -618,8 +630,8 @@
     step = norm_now / curvature
     norm_next = norm_now + step * (step * square - 2.0 * cross)
     ratio = norm_next / norm_now
-    line = lax.broadcasted_iota(jnp.int32, (8, FEATURES), 0)
-    scal_ref[...] = jnp.where(line == 0, step, ratio)
+    step_ref[...] = jnp.broadcast_to(step, step_ref.shape)
+    ratio_ref[...] = jnp.broadcast_to(ratio, ratio_ref.shape)
     finish()
 
 
@@ -647,14 +659,15 @@
         readout,
         residual.reshape(n, FEATURES),
     )
-    update, scal = pl.pallas_call(
+    update, step, ratio = pl.pallas_call(
         functools.partial(kernel, ny, nz, nx),
         out_shape=(
             jax.ShapeDtypeStruct((n, FEATURES), F32),
-            jax.ShapeDtypeStruct((8, FEATURES), F32),
+            jax.ShapeDtypeStruct((1, FEATURES), F32),
+            jax.ShapeDtypeStruct((1, FEATURES), F32),
         ),
         in_specs=[pl.BlockSpec(memory_space=pl.ANY)] * 15,
-        out_specs=(vmem, vmem),
+        out_specs=(vmem, vmem, vmem),
         scratch_shapes=[pltpu.VMEM(v.shape, v.dtype) for v in operands]
         + [
             pltpu.VMEM((FIELDS, group, nz, FEATURES), BF16),
@@ -663,23 +676,24 @@
             pltpu.VMEM((FIELDS, nz, group, FEATURES), BF16),
             pltpu.VMEM((min(4, nz), nz // min(4, nz), 16, FEATURES), BF16),
             pltpu.VMEM((2, nx, ny, six, FEATURES), BF16),
-            pltpu.VMEM((2, ny, nx, six, FEATURES), BF16),
+            pltpu.VMEM((2, nx, ny, six, FEATURES), BF16),
             pltpu.VMEM((2 * nx, n, ny * six), F32),
+            pltpu.VMEM((n, 2 * nx * ny * six), BF16),
             pltpu.VMEM((4, FEATURES, FEATURES), BF16),
             pltpu.VMEM((group * nx, 1, 128), F32),
             pltpu.VMEM((nz, 1, 128), F32),
             pltpu.VMEM((2, 1, 128), F32),
             pltpu.SemaphoreType.DMA((FIELDS, 4)),
             pltpu.SemaphoreType.DMA((4,)),
-            pltpu.SemaphoreType.DMA((2, 16)),
+            pltpu.SemaphoreType.DMA((2, 24)),
             pltpu.SemaphoreType.DMA((2, 2)),
             pltpu.SemaphoreType.DMA((15,)),
         ],
         compiler_params=pltpu.CompilerParams(
-            collective_id=0, has_side_effects=True, vmem_limit_bytes=48 * 1024 * 1024
+            collective_id=0, has_side_effects=True, vmem_limit_bytes=VMEM_BYTES
         ),
     )(*operands)
-    step, ratio = scal[0:1], scal[1:2]
+    step, ratio = (v.reshape(1, 1, 1, FEATURES) for v in (step, ratio))
     hessian_dir = direction + update.reshape(direction.shape)
     residual_new = residual - step * hessian_dir
     return (

time: 121 us -> 105 us (0.87)
  local copies, waits for them, and re-layouts: 10 us -> 1.28 us
  Pallas kernels: 108 us -> 101 us
    unnamed x30 -> x10, local copies, waits for them, and re-layouts: 10 us -> 1.28 us
    pallas_call x1, Pallas kernels: 108 us -> 101 us  [per_device(): pl.pallas_call(functools.partial(kernel, ny, nz, nx), out_shape=(jax.Shap...]
where the time goes in v3:
time: 105 us
  Pallas kernels  101 us (96%)
  other arithmetic  1.89 us (2%)
  between operations  1.34 us (1%)
  local copies, waits for them, and re-layouts  1.28 us (1%)
    pallas_call x1, Pallas kernels, per_device(): pl.pallas_call(functools.partial(kernel, ny, nz, nx), out_shape=(jax.Shap...  101 us

profile of v3, /device:TPU:1, one launch (start us, length us, event | category | flops | bytes accessed | tf_op | source)
XLA Modules:
  0.0 105.2 jit_solution(4252569582931115405)
XLA Ops:
  1.3 0.0 copy-start
  1.3 0.0 copy-start.1
  1.3 0.0 copy-start.2
  1.3 100.7 %shard_map.183 = (f32[128,384]{1,0:T(8,128)}, f32[1,384]{1,0:T(1,128)}, f32[1,384]{1,0:T(1,128)}) custom-call(bf16[128,384]{1,0:T(8,128)(2,1)} %bitcast.17, bf16[384,128]{1,0:T(8,128)(2,1)} %constant.6.clone.refs_1_, f32[128,384]{1,0:T(8,128)} %bitcast.13, bf16[6,384]{1,0:T(8,128)(2,1)} %bitcast.18, bf16[6,384]{1,0:T(8,128)(2,1)} %refs_4_.1, ...), custom_call_target="tpu_custom_call" | custom-call | tf_op jit(solution)/shard_map/pallas_call | solution.py:662
  102.0 0.0 copy-start.4
  102.0 0.6 copy-done.4
  102.6 0.0 copy-start.3
  102.7 0.6 copy-done.3
  103.3 0.0 copy-done
  103.3 0.0 copy-done.1
  103.3 0.0 copy-done.2
  103.3 1.9 %multiply_add_fusion = (f32[1,1,128,384]{3,2,1,0:T(8,128)}, f32[1,1,128,384]{3,2,1,0:T(8,128)}, f32[1,1,128,384]{3,2,1,0:T(8,128)}, f32[1,1,128,384]{3,2,1,0:T(8,128)}) fusion(f32[1,1,128,384]{3,2,1,0:T(8,128)S(1)} %copy-done, f32[384]{0:T(512)S(1)} %reduce.1, f32[1,1,128,384]{3,2,1,0:T(8,128)S(1)} %copy-done.1, f32[384]{0:T(512)S(1)} %reduce, ...), kind=kLoop, calls=%fused_computation.1 | loop fusion | flops 344064 | bytes 1575936 | tf_op jit(solution)/shard_map/add | solution.py:702
  (2 shorter events, 0.0 us)
Async XLA Ops:
  1.3 102.0 %copy-start = (f32[1,1,128,384]{3,2,1,0:T(8,128)S(1)}, f32[1,1,128,384]{3,2,1,0:T(8,128)}, u32[]{:S(2)}) copy-start(f32[1,1,128,384]{3,2,1,0:T(8,128)} %param.19) | copy-start | bytes 589828
  1.3 102.0 %copy-start.1 = (f32[1,1,128,384]{3,2,1,0:T(8,128)S(1)}, f32[1,1,128,384]{3,2,1,0:T(8,128)}, u32[]{:S(2)}) copy-start(f32[1,1,128,384]{3,2,1,0:T(8,128)} %param.18) | copy-start | bytes 589828
  1.3 102.0 %copy-start.2 = (f32[1,1,128,384]{3,2,1,0:T(8,128)S(1)}, f32[1,1,128,384]{3,2,1,0:T(8,128)}, u32[]{:S(2)}) copy-start(f32[1,1,128,384]{3,2,1,0:T(8,128)} %param.17) | copy-start | bytes 589828
  102.0 0.7 copy-start.4
  102.6 0.6 copy-start.3

commit v4 on v3

--- a/solution.py
+++ b/solution.py
@@ -172,7 +172,12 @@
         return {"lat": lat, "ens": t}
 
     z_steps = sorted(range(1, nz), key=lambda s: (-min(s, nz - s), s))
-    yc_partners = [lax.rem(me_yc + s, group) for s in range(1, group)]
+    yc_partners = [
+        lax.rem(yy + d, ny) * 2 + lax.rem(core + c, 2)
+        for d, c in sorted(
+            ((d, c) for d in range(ny) for c in (0, 1) if d or c), key=lambda p: -min(p[0], ny - p[0])
+        )
+    ]
     z_partners = [lax.rem(zz + s, nz) for s in z_steps]
     plane = [
         (lax.rem(me_yc + k, group), lax.rem(ens + t, nx))
@@ -525,6 +530,7 @@
     wout[core, ens, yy] = packed[six : 2 * six]
     gather_in.begin()
     gather_out.begin()
+    phase_two(2)
     phase_two(3)
 
     lat_inverse(4, mix(spec_slope * mix(lat_forward(1), 0), 1))
@@ -536,28 +542,6 @@
     phase_two(4)
     for gather in (gather_in, gather_out):
         gather.cross(gather.g, 0)
-    phase_two(2)
-    for i in range(max(nx, ny)):
-        for gather in (gather_in, gather_out):
-            if i < gather.nf:
-                gather.pass_on(gather.order[i])
-
-    middle = state + lon_inverse(3)
-    mixed, mixed_inverse = normalise(middle)
-    mixed_low = mixed.astype(BF16)
-
-    units = ny * six
-
-    def slope_of(co, g):
-        block = win[co, g].reshape(units, FEATURES)
-        slope_ref[co * nx + g] = gelu_parts(dot_t(mixed_low, block))[1]
-
-    slabs = gather_in.slabs()
-    slope_of(core, slabs[0])
-    arrive(("core", gather_in, 0))
-    slope_of(1 - core, slabs[0])
-    for i in range(1, min(3, nx)):
-        slope_of(core, slabs[i])
     got = received(2)
     cell_id = lax.broadcasted_iota(jnp.int32, (n, n), 1).astype(F32)
     at_a = jnp.where(got[:, 256:257] == cell_id, 1.0, 0.0)
@@ -566,6 +550,29 @@
         at_b.T.astype(BF16), got[:, 128:256].astype(BF16)
     )
 
+    for i in range(max(nx, ny)):
+        for gather in (gather_in, gather_out):
+            if i < gather.nf:
+                gather.pass_on(gather.order[i])
+
+    middle = state + lon_inverse(3)
+    mixed, mixed_inverse = normalise(middle)
+    mixed_low = mixed.astype(BF16)
+
+    units = ny * six
+
+    def slope_of(co, g):
+        block = win[co, g].reshape(units, FEATURES)
+        slope_ref[co * nx + g] = gelu_parts(dot_t(mixed_low, block))[1]
+
+    slabs = gather_in.slabs()
+    slope_of(core, slabs[0])
+    arrive(("core", gather_in, 0))
+    slope_of(1 - core, slabs[0])
+    for i in range(1, min(3, nx)):
+        slope_of(core, slabs[i])
+    tangent_middle = heading + lon_inverse(4)
+    tangent_low = norm_linear(mixed, mixed_inverse, tangent_middle).astype(BF16)
     gather_in.last()
     gather_out.last()
     for i in range(1, nx):
@@ -573,8 +580,6 @@
             slope_of(core, slabs[i])
         arrive(("core", gather_in, i))
         slope_of(1 - core, slabs[i])
-    tangent_middle = heading + lon_inverse(4)
-    tangent_low = norm_linear(mixed, mixed_inverse, tangent_middle).astype(BF16)
     for i in range(ny):
         arrive(("core", gather_out, i))
 
@@ -663,8 +668,8 @@
         functools.partial(kernel, ny, nz, nx),
         out_shape=(
             jax.ShapeDtypeStruct((n, FEATURES), F32),
-            jax.ShapeDtypeStruct((1, FEATURES), F32),
-            jax.ShapeDtypeStruct((1, FEATURES), F32),
+            jax.ShapeDtypeStruct((n, FEATURES), F32),
+            jax.ShapeDtypeStruct((n, FEATURES), F32),
         ),
         in_specs=[pl.BlockSpec(memory_space=pl.ANY)] * 15,
         out_specs=(vmem, vmem, vmem),
@@ -693,7 +698,7 @@
             collective_id=0, has_side_effects=True, vmem_limit_bytes=VMEM_BYTES
         ),
     )(*operands)
-    step, ratio = (v.reshape(1, 1, 1, FEATURES) for v in (step, ratio))
+    step, ratio = (v.reshape(direction.shape) for v in (step, ratio))
     hessian_dir = direction + update.reshape(direction.shape)
     residual_new = residual - step * hessian_dir
     return (

time: 105 us -> 100 us (0.952)
  Pallas kernels: 101 us -> 96.8 us
  local copies, waits for them, and re-layouts: 1.28 us -> 0.01 us
    pallas_call x1, Pallas kernels: 101 us -> 96.8 us  [per_device(): pl.pallas_call(functools.partial(kernel, ny, nz, nx), out_shape=(jax.Shap...]
    unnamed x10 -> x6, local copies, waits for them, and re-layouts: 1.28 us -> 0.01 us
where the time goes in v4:
time: 100 us
  Pallas kernels  96.8 us (97%)
  other arithmetic  2.05 us (2%)
  between operations  1.34 us (1%)
    pallas_call x1, Pallas kernels, per_device(): pl.pallas_call(functools.partial(kernel, ny, nz, nx), out_shape=(jax.Shap...  96.8 us
    add x1, other arithmetic, per_device(): residual_new + ratio * direction  2.05 us

profile of v4, /device:TPU:1, one launch (start us, length us, event | category | flops | bytes accessed | tf_op | source)
XLA Modules:
  0.0 100.2 jit_solution(570770822757545898)
XLA Ops:
  1.3 0.0 copy-start
  1.3 0.0 copy-start.1
  1.3 0.0 copy-start.2
  1.3 96.8 %shard_map.183 = (f32[128,384]{1,0:T(8,128)}, f32[128,384]{1,0:T(8,128)}, f32[128,384]{1,0:T(8,128)}) custom-call(bf16[128,384]{1,0:T(8,128)(2,1)} %bitcast.29, bf16[384,128]{1,0:T(8,128)(2,1)} %constant.6.clone.refs_1_, f32[128,384]{1,0:T(8,128)} %bitcast.25, bf16[6,384]{1,0:T(8,128)(2,1)} %bitcast.30, bf16[6,384]{1,0:T(8,128)(2,1)} %refs_4_.1, ...), custom_call_target="tpu_custom_call" | custom-call | tf_op jit(solution)/shard_map/pallas_call | solution.py:667
  98.1 0.0 copy-done
  98.1 0.0 copy-done.1
  98.2 0.0 copy-done.2
  98.2 2.0 %fusion = (f32[1,1,128,384]{3,2,1,0:T(8,128)}, f32[1,1,128,384]{3,2,1,0:T(8,128)}, f32[1,1,128,384]{3,2,1,0:T(8,128)}, f32[1,1,128,384]{3,2,1,0:T(8,128)}) fusion(f32[1,1,128,384]{3,2,1,0:T(8,128)S(1)} %copy-done, f32[128,384]{1,0:T(8,128)} %get-tuple-element.9, f32[1,1,128,384]{3,2,1,0:T(8,128)S(1)} %copy-done.1, f32[128,384]{1,0:T(8,128)} %get-tuple-element.7, ...), kind=kLoop, calls=%fused_computation.1 | loop fusion | flops 344064 | bytes 1966080 | tf_op jit(solution)/shard_map/add | solution.py:707
Async XLA Ops:
  1.3 96.9 %copy-start = (f32[1,1,128,384]{3,2,1,0:T(8,128)S(1)}, f32[1,1,128,384]{3,2,1,0:T(8,128)}, u32[]{:S(2)}) copy-start(f32[1,1,128,384]{3,2,1,0:T(8,128)} %param.19) | copy-start | bytes 589828
  1.3 96.9 %copy-start.1 = (f32[1,1,128,384]{3,2,1,0:T(8,128)S(1)}, f32[1,1,128,384]{3,2,1,0:T(8,128)}, u32[]{:S(2)}) copy-start(f32[1,1,128,384]{3,2,1,0:T(8,128)} %param.18) | copy-start | bytes 589828
  1.3 96.9 %copy-start.2 = (f32[1,1,128,384]{3,2,1,0:T(8,128)S(1)}, f32[1,1,128,384]{3,2,1,0:T(8,128)}, u32[]{:S(2)}) copy-start(f32[1,1,128,384]{3,2,1,0:T(8,128)} %param.17) | copy-start | bytes 589828

commit v5 on v4

--- a/solution.py
+++ b/solution.py
@@ -330,11 +330,13 @@
         sa, sb = swap_parts(a), swap_parts(b)
         upper = a * (mask_r + plain * mask_i) + b * (plain * (mask_r - mask_i)) + sb * (first * mask_i)
         lower = sa * (plain * mask_i - mask_r) - sb * plain - b * (first * mask_i)
-        out = dot_3(lat_i(), split(jnp.concatenate([upper, lower], axis=0)))
+        both_low = jnp.concatenate([upper, lower], axis=0).astype(BF16)
+        high, low = lat_i()
+        out = dot(high, both_low) + dot(low, both_low)
         s1[f] = out.reshape(group, nz, FEATURES).astype(BF16)
 
     def mix(values, which, op=dot):
-        return dot_3(split(values), (mixes[2 * which], mixes[2 * which + 1]), op)
+        return op(values.astype(BF16), mixes[which])
 
     load(bg_ref)
     state = bg_ref[...].astype(F32)
@@ -411,13 +413,12 @@
     cross_sign = jnp.where(row_real, 1.0, -1.0)
     load(spec_in_ref, spec_out_ref)
     for which, ref in ((0, spec_in_ref), (1, spec_out_ref)):
-        real_pair = split(ref[0, pl.ds(core * half, half), :])
-        imag_pair = split(ref[1, pl.ds(core * half, half), :])
-        for level in (0, 1):
-            real_part = dot(dot(spread, real_pair[level]).astype(BF16), widen)
-            imag_part = dot(dot(spread, imag_pair[level]).astype(BF16), widen)
-            dense = jnp.where(same_part, real_part, imag_part * cross_sign)
-            mixes[2 * which + level] = jnp.where(same_block, dense, 0.0).astype(BF16)
+        real_low = ref[0, pl.ds(core * half, half), :].astype(BF16)
+        imag_low = ref[1, pl.ds(core * half, half), :].astype(BF16)
+        real_part = dot(dot(spread, real_low).astype(BF16), widen)
+        imag_part = dot(dot(spread, imag_low).astype(BF16), widen)
+        dense = jnp.where(same_part, real_part, imag_part * cross_sign)
+        mixes[which] = jnp.where(same_block, dense, 0.0).astype(BF16)
 
     if far:
         arrive("quads")
@@ -464,12 +465,16 @@
 
         def begin(self):
             mine = self.block(self.g, self.f)
+            direct = [i for i in self.order[1:] if min(i, self.nf - i) == 1]
+            for i in direct:
+                push(mine, mine, self.sem(0), self.sem(self.nf - i), self.first_at(self.offset(i)))
             for i in self.order[1:]:
-                push(mine, mine, self.sem(0), self.sem(self.nf - i), self.first_at(self.offset(i)))
-                coming["first", self, self.nf - i] = (self.blocks(1), self.sem(self.nf - i))
+                coming["first", self, i] = (self.blocks(1), self.sem(i))
             self.beside(0)
             if self.nf > 1:
-                leaving.append((self.blocks(self.nf - 1), self.sem(0)))
+                leaving.append((self.blocks(len(direct)), self.sem(0)))
+            if self.nf > 2:
+                leaving.append((self.blocks(1), self.sem(24)))
             if self.ng > 1:
                 leaving.append((self.blocks(self.nf), self.sem(4)))
             if self.ng > 2:
@@ -477,6 +482,10 @@
 
         def spread(self, i):
             arrive(("first", self, i))
+            if self.nf > 2 and i != 2:
+                half = six // 2
+                ref = self.block(self.g, self.offset(i)).at[pl.ds(0 if i == 1 else half, half)]
+                push(ref, ref, self.sem(24), self.sem(2), self.first_at(self.offset(self.nf - i)))
             self.beside(i)
 
         def cross(self, g, i):
@@ -684,13 +693,13 @@
             pltpu.VMEM((2, nx, ny, six, FEATURES), BF16),
             pltpu.VMEM((2 * nx, n, ny * six), F32),
             pltpu.VMEM((n, 2 * nx * ny * six), BF16),
-            pltpu.VMEM((4, FEATURES, FEATURES), BF16),
+            pltpu.VMEM((2, FEATURES, FEATURES), BF16),
             pltpu.VMEM((group * nx, 1, 128), F32),
             pltpu.VMEM((nz, 1, 128), F32),
             pltpu.VMEM((2, 1, 128), F32),
             pltpu.SemaphoreType.DMA((FIELDS, 4)),
             pltpu.SemaphoreType.DMA((4,)),
-            pltpu.SemaphoreType.DMA((2, 24)),
+            pltpu.SemaphoreType.DMA((2, 25)),
             pltpu.SemaphoreType.DMA((2, 2)),
             pltpu.SemaphoreType.DMA((15,)),
         ],

time: 100 us -> 98.3 us (0.983)
  Pallas kernels: 96.8 us -> 94.8 us
    pallas_call x1, Pallas kernels: 96.8 us -> 94.8 us  [per_device(): pl.pallas_call(functools.partial(kernel, ny, nz, nx), out_shape=(jax.Shap...]
where the time goes in v5:
time: 98.3 us; the launch traced here: 98.2 us
  Pallas kernels  94.8 us (96%)
  other arithmetic  2.05 us (2%)
  between operations  1.34 us (1%)
    pallas_call x1, Pallas kernels, per_device(): pl.pallas_call(functools.partial(kernel, ny, nz, nx), out_shape=(jax.Shap...  94.8 us
    add x1, other arithmetic, per_device(): residual_new + ratio * direction  2.05 us

profile of v5, /device:TPU:1, one launch (start us, length us, event | category | flops | bytes accessed | tf_op | source)
XLA Modules:
  0.0 98.2 jit_solution(5999926000090125801)
XLA Ops:
  1.3 0.0 copy-start
  1.3 0.0 copy-start.1
  1.3 0.0 copy-start.2
  1.3 94.8 %shard_map.183 = (f32[128,384]{1,0:T(8,128)}, f32[128,384]{1,0:T(8,128)}, f32[128,384]{1,0:T(8,128)}) custom-call(bf16[128,384]{1,0:T(8,128)(2,1)} %bitcast.29, bf16[384,128]{1,0:T(8,128)(2,1)} %constant.6.clone.refs_1_, f32[128,384]{1,0:T(8,128)} %bitcast.25, bf16[6,384]{1,0:T(8,128)(2,1)} %bitcast.30, bf16[6,384]{1,0:T(8,128)(2,1)} %refs_4_.1, ...), custom_call_target="tpu_custom_call" | custom-call | tf_op jit(solution)/shard_map/pallas_call | solution.py:676
  96.1 0.0 copy-done
  96.1 0.0 copy-done.1
  96.1 0.0 copy-done.2
  96.1 2.0 %fusion = (f32[1,1,128,384]{3,2,1,0:T(8,128)}, f32[1,1,128,384]{3,2,1,0:T(8,128)}, f32[1,1,128,384]{3,2,1,0:T(8,128)}, f32[1,1,128,384]{3,2,1,0:T(8,128)}) fusion(f32[1,1,128,384]{3,2,1,0:T(8,128)S(1)} %copy-done, f32[128,384]{1,0:T(8,128)} %get-tuple-element.9, f32[1,1,128,384]{3,2,1,0:T(8,128)S(1)} %copy-done.1, f32[128,384]{1,0:T(8,128)} %get-tuple-element.7, ...), kind=kLoop, calls=%fused_computation.1 | loop fusion | flops 344064 | bytes 1966080 | tf_op jit(solution)/shard_map/add | solution.py:716
Async XLA Ops:
  1.3 94.8 %copy-start = (f32[1,1,128,384]{3,2,1,0:T(8,128)S(1)}, f32[1,1,128,384]{3,2,1,0:T(8,128)}, u32[]{:S(2)}) copy-start(f32[1,1,128,384]{3,2,1,0:T(8,128)} %param.19) | copy-start | bytes 589828
  1.3 94.8 %copy-start.1 = (f32[1,1,128,384]{3,2,1,0:T(8,128)S(1)}, f32[1,1,128,384]{3,2,1,0:T(8,128)}, u32[]{:S(2)}) copy-start(f32[1,1,128,384]{3,2,1,0:T(8,128)} %param.18) | copy-start | bytes 589828
  1.3 94.8 %copy-start.2 = (f32[1,1,128,384]{3,2,1,0:T(8,128)S(1)}, f32[1,1,128,384]{3,2,1,0:T(8,128)}, u32[]{:S(2)}) copy-start(f32[1,1,128,384]{3,2,1,0:T(8,128)} %param.17) | copy-start | bytes 589828
